TPU v7x, 256 devices: a whole 4x4x8 slice. The times are simulated.
256 devices in a mesh: group: 8 (over z), dev: 32 (over y, x, core).
Axes of the slice: x: 4, y: 4, z: 8, core: 2. Of those that a mesh axis runs over, the one named last changes fastest.
Arguments:
- hidden_acts: bfloat16 [32768, 11008], P(('group', 'dev')), may hold values from -6 to 6
- out_grads: bfloat16 [32768, 4096], P(('group', 'dev')), may hold values from -6 to 6
- doc_index: int32 [256, 128], P(('group', 'dev')), may hold values from 0 to 31, never falling along the last dimension, each value on 1 to 8 neighbouring positions
- proj_hidden: bfloat16 [128, 11008], replicated, may hold values from -0.0546875 to 0.0546875
- proj_grad: bfloat16 [64, 4096], replicated, may hold values from -0.09375 to 0.09375
Outputs:
- coefficients: float32 [8192, 256], P(('group', 'dev'))
- basis: float32 [256, 8192], P(None, 'dev')
Inputs may be any that keep to these rules, and one draw needn't show every extreme that they name: `doc_index`: each row holds, for one device's tokens in order, document numbers that never fall; each of the 32 documents has 1 to 8 tokens.
All inputs are finite; a program needn't handle non-finite values.
Results may differ from a plain program's by a relative error of at most 0.00035.
Values sent between devices are 32-bit elements; how exact they have to be, the bound alone decides.
A program may use at most 128 MiB of HBM per device.

v0:
```python
import math

import jax
import jax.numpy as jnp
from jax import lax
from jax.sharding import PartitionSpec as P

RANK = 256
ITERS = 2
DOC_DEV = 32


def matmul(first_factor, second_factor):
    return jnp.dot(
        first_factor,
        second_factor,
        precision=lax.Precision.HIGHEST,
        preferred_element_type=jnp.float32,
    )


def orthonormal(images):
    inner_gram = matmul(images.T, images)
    lower_factor = jnp.linalg.cholesky(inner_gram)
    return lax.linalg.triangular_solve(
        lower_factor, images, left_side=False, lower=True, transpose_a=True
    )


def projected_sides(hidden_tokens, grad_tokens, proj_hidden, proj_grad):
    hidden_side = lax.dot_general(
        hidden_tokens, proj_hidden, (((1,), (1,)), ((), ())), preferred_element_type=jnp.float32
    )
    grad_side = lax.dot_general(
        grad_tokens, proj_grad, (((1,), (1,)), ((), ())), preferred_element_type=jnp.float32
    )
    return (hidden_side, grad_side)


def document_rows(hidden_side, grad_side, token_docs):
    one_hot = (token_docs[None, :] == jnp.arange(DOC_DEV, dtype=jnp.int32)[:, None]).astype(
        jnp.float32
    )
    weighted = one_hot[:, None, :] * grad_side.T[None, :, :]
    outer_sums = matmul(weighted.reshape(-1, token_docs.shape[0]), hidden_side)
    width_total = grad_side.shape[1] * hidden_side.shape[1]
    return outer_sums.reshape(DOC_DEV, width_total) * (1.0 / math.sqrt(width_total))


def gram_basis(summed_gram):
    group_basis = orthonormal(summed_gram[:, :RANK])
    for repeat in range(ITERS):
        group_basis = orthonormal(matmul(summed_gram, group_basis))
    return group_basis


def on_device(hidden_acts, out_grads, doc_index, proj_hidden, proj_grad):
    hidden_side, grad_side = projected_sides(hidden_acts, out_grads, proj_hidden, proj_grad)
    width_total = grad_side.shape[1] * hidden_side.shape[1]
    doc_block = document_rows(hidden_side, grad_side, doc_index[0])
    column_block = lax.all_to_all(doc_block, "dev", split_axis=1, concat_axis=0, tiled=True)
    summed_gram = lax.psum(matmul(column_block, column_block.T), "dev")
    group_basis = gram_basis(summed_gram)
    sketch = matmul(group_basis.T, column_block)
    stacked = lax.all_gather(sketch, "group", axis=0, tiled=True)

    def merged_apply(factor):
        owned_rows = lax.psum_scatter(
            matmul(stacked, factor), "dev", scatter_dimension=0, tiled=True
        )
        return lax.all_gather(owned_rows, "dev", axis=0, tiled=True)

    merged_basis = orthonormal(merged_apply(stacked[:RANK].T))
    for repeat in range(ITERS):
        merged_basis = orthonormal(merged_apply(matmul(stacked.T, merged_basis)))
    merged = matmul(merged_basis.T, stacked)
    squares = lax.psum(jnp.sum(merged * merged, axis=1), "dev")
    factors = 1.0 / jnp.sqrt(squares / width_total + 1e-06)
    basis_block = merged * factors[:, None]
    root_width = math.sqrt(width_total)
    summed = lax.psum_scatter(
        matmul(column_block, basis_block.T), "dev", scatter_dimension=0, tiled=True
    )
    coefficients = summed / root_width
    return (coefficients, basis_block)


def solution(mesh):
    return jax.shard_map(
        on_device,
        mesh=mesh,
        in_specs=(
            P(("group", "dev"), None),
            P(("group", "dev"), None),
            P(("group", "dev"), None),
            P(),
            P(),
        ),
        out_specs=(P(("group", "dev"), None), P(None, "dev")),
        check_vma=False,
    )
```

profile of v0, /device:TPU:1, one launch (start us, length us, event | category | flops | bytes accessed | tf_op | source)
XLA Modules:
  0.0 1246.5 jit_solution(7119634385873738465)
XLA Ops:
  10.0 2.7 fusion.110
  12.7 2.0 convolution_multiply_fusion
  14.7 2.5 mul.44
  19.1 25.6 %all_to_all.16 = f32[32,32,256]{2,0,1:T(8,128)S(1)} all-to-all(f32[32,32,256]{2,0,1:T(8,128)S(1)} %copy.14), channel_id=1, replica_groups=mesh['group'=8,'dev'=32] {'dev'}, dimensions={1} | all-to-all | bytes 2097152 | tf_op jit(solution)/shard_map/all_to_all | solution.py:61
  45.7 5.1 fusion.111
  51.0 120.7 %all-reduce.3.cloned.1.call-done = f32[1024,1024]{1,0:T(8,128)} async-done(((f32[1024,1024]{1,0:T(8,128)}), f32[1024,1024]{1,0:T(8,128)}) %all-reduce.3.cloned.1.call-update) | async-done | bytes 4194320 | tf_op jit(solution)/shard_map/psum | solution.py:62
  171.8 3.6 fusion.18
  176.3 11.7 cholesky.298
  188.0 9.8 custom-call.23
  200.0 11.7 cholesky.315
  214.0 3.9 while.12
  218.0 19.7 %custom-call.24 = f32[2,128,128]{1,2,0:T(8,128)S(1)} custom-call(f32[2,128,128]{2,1,0:T(8,128)S(1)} %get-tuple-element.45), custom_call_target="InvertDiagBlocksLowerTriangular" | custom-call | tf_op jit(solution)/shard_map/triangular_solve/custom-call.0 | solution.py:25
  239.4 2.0 convolution_subtract_fusion.5
  242.0 5.8 fusion.20
  251.6 11.7 cholesky.332
  263.4 9.8 custom-call.25
  275.4 11.7 cholesky.349
  289.9 4.0 while.13
  293.9 19.7 %custom-call.26 = f32[2,128,128]{1,2,0:T(8,128)S(1)} custom-call(f32[2,128,128]{2,1,0:T(8,128)S(1)} %get-tuple-element.46), custom_call_target="InvertDiagBlocksLowerTriangular" | custom-call | tf_op jit(solution)/shard_map/triangular_solve/custom-call.0 | solution.py:25
  315.2 2.0 convolution_subtract_fusion.4
  317.9 5.3 fusion.24
  327.0 11.7 cholesky.366
  338.8 9.8 custom-call.27
  350.8 11.7 cholesky.383
  365.6 4.1 while.14
  369.8 19.7 %custom-call.28 = f32[2,128,128]{1,2,0:T(8,128)S(1)} custom-call(f32[2,128,128]{2,1,0:T(8,128)S(1)} %get-tuple-element.47), custom_call_target="InvertDiagBlocksLowerTriangular" | custom-call | tf_op jit(solution)/shard_map/triangular_solve/custom-call.0 | solution.py:25
  391.2 2.0 convolution_subtract_fusion.3
  395.7 37.2 %all-gather.5.cloned.1.call-done = f32[2048,256]{1,0:T(8,128)} async-done(((f32[256,256]{1,0:T(8,128)}), f32[2048,256]{1,0:T(8,128)}) %all-gather.5.cloned.1.call-update) | async-done | bytes 2097168 | tf_op jit(solution)/shard_map/all_gather | solution.py:65
  432.9 4.7 fusion.38
  437.7 87.2 %reduce-scatter.5.cloned.1.call-done = f32[64,256]{1,0:T(8,128)} async-done(((f32[2048,256]{1,0:T(8,128)}), f32[64,256]{1,0:T(8,128)}) %reduce-scatter.5.cloned.1.call-update) | async-done | bytes 65552 | tf_op jit(solution)/shard_map/reduce_scatter | solution.py:68
  525.2 52.5 %all-gather.7.cloned.1.call-done = f32[2048,256]{1,0:T(8,128)} async-done(((f32[64,256]{1,0:T(8,128)}), f32[2048,256]{1,0:T(8,128)}) %all-gather.7.cloned.1.call-update) | async-done | bytes 2097168 | tf_op jit(solution)/shard_map/all_gather | solution.py:71
  577.7 5.7 fusion.114
  584.3 11.7 cholesky.400
  596.0 9.8 custom-call.29
  608.0 12.1 cholesky.417
  622.8 3.9 while.15
  626.7 19.7 %custom-call.30 = f32[2,128,128]{1,2,0:T(8,128)S(1)} custom-call(f32[2,128,128]{2,1,0:T(8,128)S(1)} %get-tuple-element.48), custom_call_target="InvertDiagBlocksLowerTriangular" | custom-call | tf_op jit(solution)/shard_map/triangular_solve/custom-call.4 | solution.py:25
  646.4 2.4 fusion.16
  651.8 3.6 fusion
  655.4 3.1 fusion.115
  658.6 83.8 %reduce-scatter.7.cloned.1.call-done = f32[64,256]{1,0:T(8,128)} async-done(((f32[2048,256]{1,0:T(8,128)}), f32[64,256]{1,0:T(8,128)}) %reduce-scatter.7.cloned.1.call-update) | async-done | bytes 65552 | tf_op jit(solution)/shard_map/reduce_scatter | solution.py:68
  742.6 52.5 %all-gather.9.cloned.1.call-done = f32[2048,256]{1,0:T(8,128)} async-done(((f32[64,256]{1,0:T(8,128)}), f32[2048,256]{1,0:T(8,128)}) %all-gather.9.cloned.1.call-update) | async-done | bytes 2097168 | tf_op jit(solution)/shard_map/all_gather | solution.py:71
  795.1 5.7 fusion.116
  801.7 11.7 cholesky.434
  813.5 9.8 custom-call.31
  825.5 12.1 cholesky.451
  840.2 3.9 while.16
  844.2 19.7 %custom-call.32 = f32[2,128,128]{1,2,0:T(8,128)S(1)} custom-call(f32[2,128,128]{2,1,0:T(8,128)S(1)} %get-tuple-element.49), custom_call_target="InvertDiagBlocksLowerTriangular" | custom-call | tf_op jit(solution)/shard_map/triangular_solve/custom-call.4 | solution.py:25
  863.9 2.4 fusion.14
  869.3 3.6 fusion.4
  872.9 3.1 fusion.117
  876.1 83.8 %reduce-scatter.9.cloned.1.call-done = f32[64,256]{1,0:T(8,128)} async-done(((f32[2048,256]{1,0:T(8,128)}), f32[64,256]{1,0:T(8,128)}) %reduce-scatter.9.cloned.1.call-update) | async-done | bytes 65552 | tf_op jit(solution)/shard_map/reduce_scatter | solution.py:68
  960.1 52.7 %all-gather.11.cloned.1.call-done = f32[2048,256]{1,0:T(8,128)} async-done(((f32[64,256]{1,0:T(8,128)}), f32[2048,256]{1,0:T(8,128)}) %all-gather.11.cloned.1.call-update) | async-done | bytes 2097168 | tf_op jit(solution)/shard_map/all_gather | solution.py:71
  1012.8 5.7 fusion.118
  1019.3 11.7 cholesky.468
  1031.1 9.8 custom-call.33
  1043.1 11.9 cholesky.485
  1057.6 3.9 while.17
  1061.6 19.7 %custom-call.34 = f32[2,128,128]{1,2,0:T(8,128)S(1)} custom-call(f32[2,128,128]{2,1,0:T(8,128)S(1)} %get-tuple-element.50), custom_call_target="InvertDiagBlocksLowerTriangular" | custom-call | tf_op jit(solution)/shard_map/triangular_solve/custom-call.4 | solution.py:25
  1081.3 2.4 fusion.12
  1086.7 3.5 multiply_reduce_fusion
  1090.2 62.3 %psum.15 = f32[256]{0:T(256)S(1)} all-reduce(f32[256]{0:T(256)S(1)} %get-tuple-element.151), channel_id=1, replica_groups=mesh['group'=8,'dev'=32] {'dev'}, use_global_device_ids=true, to_apply=%region_9.13 | all-reduce | flops 256 | bytes 2048 | tf_op jit(solution)/shard_map/psum | solution.py:77
  1152.6 3.2 fusion.119
  1156.6 81.7 %reduce-scatter.11.cloned.1.call-done = f32[32,256]{1,0:T(8,128)} async-done(((f32[1024,256]{1,0:T(8,128)}), f32[32,256]{1,0:T(8,128)}) %reduce-scatter.11.cloned.1.call-update) | async-done | bytes 32784 | tf_op jit(solution)/shard_map/reduce_scatter | solution.py:81
  (184 shorter events, 82.3 us)
Async XLA Ops:
  7.2 2.9 copy-start
  7.2 164.6 %all-reduce.3.cloned.1.call-start = ((), (), s32[]{:S(2)}) async-start(), calls=%async_computation.5 | async-start | bytes 8388608 | tf_op jit(solution)/shard_map/psum | solution.py:62
  44.7 1.1 copy-start.4
  50.8 382.1 %all-gather.5.cloned.1.call-start = ((), (), s32[]{:S(2)}) async-start(), calls=%async_computation.6 | async-start | bytes 2359296 | tf_op jit(solution)/shard_map/all_gather | solution.py:65
  175.6 0.7 copy-start.11
  247.8 1.0 copy-start.10
  250.9 0.7 copy-start.12
  323.2 1.0 copy-start.9
  326.3 0.7 copy-start.13
  389.4 4.5 copy-start.5
  395.7 129.3 %reduce-scatter.5.cloned.1.call-start = ((), (), s32[]{:S(2)}) async-start(), calls=%async_computation.7 | async-start | bytes 2162688 | tf_op jit(solution)/shard_map/reduce_scatter | solution.py:68
  437.7 140.0 %all-gather.7.cloned.1.call-start = ((), (), s32[]{:S(2)}) async-start(), calls=%async_computation.8 | async-start | bytes 2162688 | tf_op jit(solution)/shard_map/all_gather | solution.py:71
  524.9 217.4 %reduce-scatter.7.cloned.1.call-start = ((), (), s32[]{:S(2)}) async-start(), calls=%async_computation.9 | async-start | bytes 2162688 | tf_op jit(solution)/shard_map/reduce_scatter | solution.py:68
  583.6 0.7 copy-start.14
  646.4 2.5 copy-start.7
  648.9 2.9 copy-start.1
  658.5 136.6 %all-gather.9.cloned.1.call-start = ((), (), s32[]{:S(2)}) async-start(), calls=%async_computation.10 | async-start | bytes 2162688 | tf_op jit(solution)/shard_map/all_gather | solution.py:71
  742.4 217.4 %reduce-scatter.9.cloned.1.call-start = ((), (), s32[]{:S(2)}) async-start(), calls=%async_computation.11 | async-start | bytes 2162688 | tf_op jit(solution)/shard_map/reduce_scatter | solution.py:68
  801.0 0.7 copy-start.15
  863.9 2.5 copy-start.8
  866.3 2.9 copy-start.2
  876.0 136.8 %all-gather.11.cloned.1.call-start = ((), (), s32[]{:S(2)}) async-start(), calls=%async_computation.12 | async-start | bytes 2162688 | tf_op jit(solution)/shard_map/all_gather | solution.py:71
  959.9 278.5 %reduce-scatter.11.cloned.1.call-start = ((), (), s32[]{:S(2)}) async-start(), calls=%async_computation.13 | async-start | bytes 1081344 | tf_op jit(solution)/shard_map/reduce_scatter | solution.py:81
  1018.6 0.7 copy-start.16
  1081.3 2.5 copy-start.6
  1083.7 2.9 copy-start.3
Sparse Core Ops, SparseCore 0:
  50.9 120.7 all-reduce.2
  395.8 37.0 all-gather.4
  437.8 87.0 reduce-scatter.4
  527.3 50.3 all-gather.6
  658.7 83.6 reduce-scatter.6
  744.8 50.3 all-gather.8
  876.1 83.6 reduce-scatter.8
  962.4 50.3 all-gather.10
  1155.9 82.3 reduce-scatter.10
where the time goes:
time: 1250 us
  waiting for transfers between devices  652 us (52%)
  other arithmetic  329 us (26%)
  matrix products  116 us (9%)
  blocking collectives  87.8 us (7%)
  local copies, waits for them, and re-layouts  37.1 us (3%)
  between operations  23.1 us (2%)
    reduce_scatter x3, waiting for transfers between devices, merged_apply(): lax.psum_scatter(matmul(stacked, factor), 'dev', scatter_dimension=0, til...  255 us
    another operation x41, other arithmetic, orthonormal(): lower_factor = jnp.linalg.cholesky(inner_gram)  208 us
    all_gather x3, waiting for transfers between devices, merged_apply(): return lax.all_gather(owned_rows, 'dev', axis=0, tiled=True)  158 us
    psum x1, waiting for transfers between devices, on_device(): summed_gram = lax.psum(matmul(column_block, column_block.T), 'dev')  121 us
    another operation x13, other arithmetic, orthonormal(): lax.linalg.triangular_solve(lower_factor, images, left_side=False, lower=...  118 us
    reduce_scatter x1, waiting for transfers between devices, on_device(): lax.psum_scatter(matmul(column_block, basis_block.T), 'dev', scatter_dime...  81.7 us
    dot_general x18, matrix products, matmul(): jnp.dot(first_factor, second_factor, precision=lax.Precision.HIGHEST, pre...  69.2 us
    psum x1, blocking collectives, on_device(): squares = lax.psum(jnp.sum(merged * merged, axis=1), 'dev')  62.3 us
  transfers between devices with their start and end apart: 9, of which 9 were waited for; matrix products, arithmetic and copies ran while one was open for 0% of the time, Pallas kernels for 0%

commit v1 on v0

v1 whole, which is shorter than its diff:
```python
import functools
import math

import jax
import jax.numpy as jnp
from jax import lax
from jax.experimental import pallas as pl
from jax.experimental.pallas import tpu as pltpu
from jax.sharding import PartitionSpec as P

RANK = 256
ITERS = 2
DOC_DEV = 32
F32 = jnp.float32
BF = jnp.bfloat16
MESH = pl.DeviceIdType.MESH
VM = pl.BlockSpec(memory_space=pltpu.VMEM)
HI = lax.Precision.HIGHEST


def split3(x):
    h=x.astype(BF); r=x-h.astype(F32); m=r.astype(BF); l=(r-m.astype(F32)).astype(BF)
    return h,m,l

def panel_factor(P, p, nb):
    n=P.shape[1]
    lane=lax.broadcasted_iota(jnp.int32,(nb,n),1)
    row=lax.broadcasted_iota(jnp.int32,(nb,n),0)
    rowb=lax.broadcasted_iota(jnp.int32,(nb,128),0)
    S=jnp.ones((nb,128),F32)
    for leaf in range(nb//8):
        c0=nb*p+8*leaf
        B=[jnp.broadcast_to(P[:,c0+j:c0+j+1],(nb,128)) for j in range(8)]
        for k in range(8):
            rk=8*leaf+k
            pv=B[k][rk:rk+1,:]
            rp=1.0/pv
            f=jnp.where(rowb>rk,B[k]*rp,0.0)
            for j in range(k+1,8):
                B[j]=B[j]-f*B[j][rk:rk+1,:]
            S=jnp.where(rowb==rk,lax.rsqrt(pv),S)
            hit=lane==(c0+k)
            prow=jnp.where(hit[0:1],1.0,P[rk:rk+1,:])
            ff=jnp.concatenate([f]*(n//128),axis=1)
            P=jnp.where(hit&(row>rk),0.0,jnp.where(hit&(row==rk),1.0,P))-ff*prow
    return P*jnp.concatenate([S]*(n//128),axis=1)

def chol_inv_body(A, nb=32):
    n=A.shape[0]
    for p in range(n//nb):
        r0=nb*p; r1=r0+nb
        R=panel_factor(A[r0:r1,:],p,nb)
        A[r0:r1,:]=R
        if r1<n:
            plane=lax.broadcasted_iota(jnp.int32,(nb,n),1); prow=lax.broadcasted_iota(jnp.int32,(nb,n),0)
            R=jnp.where((plane>=r0)&(plane<r1)&(plane-r0>prow),0.0,R)
            h,m,l=split3(R)
            rhs=jnp.concatenate([h,m,h,l,m,h],axis=0)
            lh,lm,ll=h[:,r1:],m[:,r1:],l[:,r1:]
            lhs=jnp.concatenate([lh,lh,lm,lh,lm,ll],axis=0)
            upd=lax.dot_general(lhs,rhs,(((0,),(0,)),((),())),preferred_element_type=F32)
            lane=lax.broadcasted_iota(jnp.int32,(n-r1,n),1)
            T=A[r1:,:]
            A[r1:,:]=jnp.where((lane>=r0)&(lane<r1),0.0,T)-upd

def chol_kernel(nb,k_ref,w_ref,A):
    A[...]=k_ref[...]
    chol_inv_body(A,nb)
    n=A.shape[0]
    r=lax.broadcasted_iota(jnp.int32,(n,n),0); c=lax.broadcasted_iota(jnp.int32,(n,n),1)
    w_ref[...]=jnp.where(c<=r,A[...],0.0)

def chol_inv(K,nb=32):
    n=K.shape[0]
    return pl.pallas_call(functools.partial(chol_kernel,nb),out_shape=jax.ShapeDtypeStruct((n,n),F32),
      in_specs=[pl.BlockSpec(memory_space=pltpu.VMEM)],out_specs=pl.BlockSpec(memory_space=pltpu.VMEM),
      scratch_shapes=[pltpu.VMEM((n,n),F32)],compiler_params=pltpu.CompilerParams(vmem_limit_bytes=32<<20))(K)


def barrier(peers):
    b=pltpu.get_barrier_semaphore()
    for q in peers: pl.semaphore_signal(b,inc=1,device_id=q,device_id_type=MESH)
    pl.semaphore_wait(b,len(peers))

def rcopy(src,dst,ss,rs,dev):
    return pltpu.make_async_remote_copy(src_ref=src,dst_ref=dst,send_sem=ss,recv_sem=rs,device_id=dev,device_id_type=MESH)

def ag_kernel(x_ref,out,ss,rs,ls):
    g=lax.axis_index("group"); me=lax.axis_index("dev")
    core=lax.rem(me,2); x=lax.rem(me//2,4); y=me//8
    hr=x_ref.shape[0]//2
    def did(yy,xx,cc): return (yy*4+xx)*2+cc
    xs=[lax.rem(x+k,4) for k in (1,2,3)]; ys=[lax.rem(y+k,4) for k in (1,2,3)]
    peers=[(g,did(y,a,core)) for a in xs]+[(g,did(b,x,core)) for b in ys]+[(g,did(y,x,1-core))]
    sib=(g,did(y,x,1-core))
    barrier(peers)
    lc=pltpu.make_async_copy(x_ref,out.at[me],ls); lc.start()
    H=[pl.ds(0,hr),pl.ds(hr,hr)]
    sends=[]
    def send(src,owner,h,dev,slot):
        c=rcopy(src,out.at[owner,H[h]],ss.at[len(sends)],rs.at[owner,h],dev); c.start(); sends.append(c)
    for k in range(3):
        send(x_ref.at[H[0]],me,0,(g,did(y,xs[k],core)),0)
        send(x_ref.at[H[1]],me,1,(g,did(ys[k],x,core)),0)
    for k in range(3):
        send(x_ref.at[H[0]],me,0,(g,did(ys[k],x,core)),0)
        send(x_ref.at[H[1]],me,1,(g,did(y,xs[k],core)),0)
    for h in range(2): send(x_ref.at[H[h]],me,h,sib,0)
    def wait(owner,h):
        rcopy(out.at[owner,H[h]],out.at[owner,H[h]],ss.at[0],rs.at[owner,h],sib).wait_recv()
    order=(0,2,1)
    for k in order:
        ox=did(y,xs[k],core); oy=did(ys[k],x,core)
        wait(ox,0)
        for q in range(3): send(out.at[ox,H[0]],ox,0,(g,did(ys[q],x,core)),0)
        send(out.at[ox,H[0]],ox,0,sib,0)
        wait(oy,1)
        for q in range(3): send(out.at[oy,H[1]],oy,1,(g,did(y,xs[q],core)),0)
        send(out.at[oy,H[1]],oy,1,sib,0)
    for k in order:
        ox=did(y,xs[k],core); oy=did(ys[k],x,core)
        wait(oy,0); send(out.at[oy,H[0]],oy,0,sib,0)
        wait(ox,1); send(out.at[ox,H[1]],ox,1,sib,0)
    for k in order:
        for q in order:
            o=did(ys[k],xs[q],core)
            for h in range(2):
                wait(o,h); send(out.at[o,H[h]],o,h,sib,0)
    lc.wait()
    for yy in range(4):
        for xx in range(4):
            for h in range(2): wait(did(yy,xx,1-core),h)
    for c in sends: c.wait_send()

def ag_dev(x,cid):
    r,c=x.shape
    return pl.pallas_call(ag_kernel,out_shape=jax.ShapeDtypeStruct((32,r,c),F32),in_specs=[VM],out_specs=VM,
      scratch_shapes=[pltpu.SemaphoreType.DMA((80,)),pltpu.SemaphoreType.DMA((32,2)),pltpu.SemaphoreType.DMA],
      compiler_params=pltpu.CompilerParams(collective_id=cid,has_side_effects=True,vmem_limit_bytes=48<<20))(x)

def ar_kernel(axis,n,u_ref,out,rbuf,ss,rs,ss2,rs2):
    g=lax.axis_index("group"); d=lax.axis_index("dev")
    me=g if axis=="group" else d
    def dev(i): return (i,d) if axis=="group" else (g,i)
    r=u_ref.shape[0]//n
    b=pltpu.get_barrier_semaphore()
    def sig(k,_):
        pl.semaphore_signal(b,inc=1,device_id=dev(lax.rem(me+k,n)),device_id_type=MESH); return 0
    lax.fori_loop(1,n,sig,0)
    pl.semaphore_wait(b,n-1)
    def rows(i): return pl.ds(pl.multiple_of(i*r,8),r)
    def s1(k,_):
        q=lax.rem(me+k,n)
        rcopy(u_ref.at[rows(q)],rbuf.at[n-k],ss.at[k],rs.at[n-k],dev(q)).start(); return 0
    lax.fori_loop(1,n,s1,0)
    def w1(k,acc):
        rcopy(rbuf.at[k],rbuf.at[k],ss.at[k],rs.at[k],dev(me)).wait_recv()
        return acc+rbuf[k]
    acc=lax.fori_loop(1,n,w1,u_ref[rows(me),:])
    out[rows(me),:]=acc
    def s2(k,_):
        q=lax.rem(me+k,n)
        rcopy(out.at[rows(me)],out.at[rows(me)],ss2.at[k],rs2.at[n-k],dev(q)).start(); return 0
    lax.fori_loop(1,n,s2,0)
    def w2(k,_):
        q=lax.rem(me+k,n)
        rcopy(out.at[rows(q)],out.at[rows(q)],ss.at[k],rs2.at[k],dev(me)).wait_recv(); return 0
    lax.fori_loop(1,n,w2,0)
    def w3(k,_):
        rcopy(u_ref.at[rows(0)],rbuf.at[k],ss.at[k],rs.at[k],dev(me)).wait_send()
        rcopy(u_ref.at[rows(0)],rbuf.at[k],ss2.at[k],rs.at[k],dev(me)).wait_send()
        return 0
    lax.fori_loop(1,n,w3,0)

def ar(u,axis,n,cid):
    R,c=u.shape
    S=pltpu.SemaphoreType.DMA((n,))
    return pl.pallas_call(functools.partial(ar_kernel,axis,n),out_shape=jax.ShapeDtypeStruct((R,c),F32),in_specs=[VM],out_specs=VM,
      scratch_shapes=[pltpu.VMEM((n,R//n,c),F32),S,S,S,S],
      compiler_params=pltpu.CompilerParams(collective_id=cid,has_side_effects=True,vmem_limit_bytes=48<<20))(u)


def rs_kernel(n, u_ref, out, rbuf, ss, rs):
    g = lax.axis_index("group"); me = lax.axis_index("dev")
    r = u_ref.shape[0] // n
    b = pltpu.get_barrier_semaphore()
    def sig(k, _):
        pl.semaphore_signal(b, inc=1, device_id=(g, lax.rem(me + k, n)), device_id_type=MESH); return 0
    lax.fori_loop(1, n, sig, 0)
    pl.semaphore_wait(b, n - 1)
    def rows(i): return pl.ds(pl.multiple_of(i * r, 8), r)
    def s1(k, _):
        q = lax.rem(me + k, n)
        rcopy(u_ref.at[rows(q)], rbuf.at[n - k], ss.at[k], rs.at[n - k], (g, q)).start(); return 0
    lax.fori_loop(1, n, s1, 0)
    def w1(k, acc):
        rcopy(rbuf.at[k], rbuf.at[k], ss.at[k], rs.at[k], (g, me)).wait_recv()
        return acc + rbuf[k]
    out[...] = lax.fori_loop(1, n, w1, u_ref[rows(me), :])
    def w3(k, _):
        rcopy(u_ref.at[rows(0)], rbuf.at[k], ss.at[k], rs.at[k], (g, me)).wait_send(); return 0
    lax.fori_loop(1, n, w3, 0)


def rs_dev(u, n, cid):
    R, c = u.shape
    S = pltpu.SemaphoreType.DMA((n,))
    return pl.pallas_call(functools.partial(rs_kernel, n), out_shape=jax.ShapeDtypeStruct((R // n, c), F32), in_specs=[VM], out_specs=VM,
      scratch_shapes=[pltpu.VMEM((n, R // n, c), F32), S, S],
      compiler_params=pltpu.CompilerParams(collective_id=cid, has_side_effects=True, vmem_limit_bytes=48 << 20))(u)


def mm(a, b, ca=1, cb=0):
    return lax.dot_general(a, b, (((ca,), (cb,)), ((), ())), precision=HI, preferred_element_type=F32)


def on_device(hidden_acts, out_grads, doc_index, proj_hidden, proj_grad):
    g = lax.axis_index("group"); d = lax.axis_index("dev")
    hs = lax.dot_general(hidden_acts, proj_hidden, (((1,), (1,)), ((), ())), preferred_element_type=F32)
    gt = lax.dot_general(proj_grad, out_grads, (((1,), (1,)), ((), ())), preferred_element_type=F32)
    tok = jnp.concatenate([hs, gt, jnp.broadcast_to(doc_index.astype(F32), (8, 128))], axis=0)
    al = ag_dev(tok, 1)
    H = al[:, :128, :]
    Gt = al[:, 128:192, :]
    O = (al[:, 192, None, :] == jnp.arange(DOC_DEV, dtype=F32)[None, :, None]).astype(F32)
    own = (doc_index == jnp.arange(DOC_DEV, dtype=jnp.int32)[:, None]).astype(F32)
    scale = 1.0 / 8192.0
    gsel = lax.dynamic_slice(Gt, (0, 2 * d, 0), (32, 2, 128)) * (1.0 / math.sqrt(8192))
    W = (O[:, :, None, :] * gsel[:, None, :, :]).reshape(32, 64, 128)
    M = lax.dot_general(W, H, (((2,), (1,)), ((0,), (0,))), precision=HI, preferred_element_type=F32).reshape(1024, 256)
    A = mm(hs, H.reshape(4096, 128), 1, 1)
    B = lax.dot_general(gt, Gt, (((0,), (1,)), ((), ())), precision=HI, preferred_element_type=F32).reshape(128, 4096)
    T = mm(own, A * B).reshape(32, 32, 128)
    Gown = lax.dot_general(T, O, (((2,), (2,)), ((1,), (0,))), precision=HI, preferred_element_type=F32)
    Gown = Gown.transpose(1, 0, 2).reshape(32, 1024) * scale
    Yo = Gown[:, :RANK]
    for it in range(ITERS + 1):
        Y = ag_dev(Yo, 2 + it).reshape(1024, RANK)
        Wi = chol_inv(mm(Y, Y, 0, 0))
        Q = mm(Y, Wi, 1, 1)
        if it < ITERS:
            Yo = mm(Gown, Q)
    S = mm(Q, M, 0, 0)
    X = ar(jnp.where(g == 0, S, 0.0), "group", 8, 5).T
    for it in range(ITERS + 1):
        U = ar(mm(S, X), "dev", 32, 6 + 3 * it)
        K = ar(mm(U, U, 0, 0), "group", 8, 7 + 3 * it)
        V = ar(mm(S, U, 0, 0), "group", 8, 8 + 3 * it)
        Wi = chol_inv(K)
        X = mm(V, Wi, 1, 1)
    merged = X.T
    sq = jnp.broadcast_to(jnp.sum(merged * merged, axis=1)[None, None, :], (32, 8, 256))
    cf = mm(M, X).reshape(32, 32, 256)
    red = rs_dev(jnp.concatenate([cf, sq], axis=1).reshape(1280, 256), 32, 20)
    factors = 1.0 / jnp.sqrt(red[32] / 8192.0 + 1e-06)
    return (red[:32] * (factors / math.sqrt(8192))[None, :], merged * factors[:, None])


def solution(mesh):
    return jax.shard_map(
        on_device,
        mesh=mesh,
        in_specs=(
            P(("group", "dev"), None),
            P(("group", "dev"), None),
            P(("group", "dev"), None),
            P(),
            P(),
        ),
        out_specs=(P(("group", "dev"), None), P(None, "dev")),
        check_vma=False,
    )
```

time: 1250 us -> 380 us (0.30)
  waiting for transfers between devices: 652 us -> 0 us
  other arithmetic: 329 us -> 1.34 us
  Pallas kernels: 0 us -> 322 us
  blocking collectives: 87.8 us -> 0 us
  matrix products: 116 us -> 37.5 us
  local copies, waits for them, and re-layouts: 37.1 us -> 9.64 us
  between operations: 23.1 us -> 1.6 us
    reduce_scatter x4 -> x0, waiting for transfers between devices: 337 us -> none  [the longest x3 255 us: merged_apply(): lax.psum_scatter(matmul(stacked, factor), 'dev', scatter_dimension=0, til...]
    another operation x54 -> x0, other arithmetic: 326 us -> none  [the longest x41 208 us: orthonormal(): lower_factor = jnp.linalg.cholesky(inner_gram)]
    pallas_call x0 -> x21, Pallas kernels: none -> 322 us  [the longest x10 191 us: ar(): pl.pallas_call(functools.partial(ar_kernel, axis, n), out_shape=jax.Shape...]
    all_gather x4 -> x0, waiting for transfers between devices: 195 us -> none  [the longest x3 158 us: merged_apply(): return lax.all_gather(owned_rows, 'dev', axis=0, tiled=True)]
    psum x1 -> x0, waiting for transfers between devices: 121 us -> none  [on_device(): summed_gram = lax.psum(matmul(column_block, column_block.T), 'dev')]
    psum x1 -> x0, blocking collectives: 62.3 us -> none  [on_device(): squares = lax.psum(jnp.sum(merged * merged, axis=1), 'dev')]
    another operation x30 -> x0, matrix products: 42.1 us -> none  [the longest x18 29.2 us: orthonormal(): lax.linalg.triangular_solve(lower_factor, images, left_side=False, lower=...]
    dot_general x20 -> x29, matrix products: 73.8 us -> 37.5 us  [the longest x24 25.7 us: mm(): lax.dot_general(a, b, (((ca,), (cb,)), ((), ())), precision=HI, preferred...]
  transfers between devices with their start and end apart: 9 -> 0, of which waited for: 9 -> 0; matrix products, arithmetic and copies ran while one was open for 0% -> 0% of each run, Pallas kernels for 0% -> 0%
where the time goes in v1:
time: 380 us; the launch traced here: 372 us
  Pallas kernels  322 us (85%)
  matrix products  37.5 us (10%)
  local copies, waits for them, and re-layouts  9.64 us (3%)
    pallas_call x10, Pallas kernels, ar(): pl.pallas_call(functools.partial(ar_kernel, axis, n), out_shape=jax.Shape...  191 us
    pallas_call x4, Pallas kernels, ag_dev(): pl.pallas_call(ag_kernel, out_shape=jax.ShapeDtypeStruct((32, r, c), F32)...  58.6 us
    pallas_call x6, Pallas kernels, chol_inv(): pl.pallas_call(functools.partial(chol_kernel, nb), out_shape=jax.ShapeDty...  47.1 us
    dot_general x24, matrix products, mm(): lax.dot_general(a, b, (((ca,), (cb,)), ((), ())), precision=HI, preferred...  25.7 us
    pallas_call x1, Pallas kernels, rs_dev(): pl.pallas_call(functools.partial(rs_kernel, n), out_shape=jax.ShapeDtypeS...  25.6 us

profile of v1, /device:TPU:1, one launch (start us, length us, event | category | flops | bytes accessed | tf_op | source)
XLA Modules:
  0.0 372.5 jit_solution(15710987629520497481)
XLA Ops:
  0.6 0.0 copy-start
  0.6 0.0 copy-start.2
  0.7 1.8 copy-done
  2.4 2.7 fusion.13
  5.2 0.5 fusion.14
  5.7 21.4 %shard_map.68 = f32[32,200,128]{2,1,0:T(8,128)S(1)} custom-call(f32[200,128]{1,0:T(8,128)S(1)} %pad_maximum_fusion.1.x_ref), custom_call_target="tpu_custom_call" | custom-call | tf_op jit(solution)/shard_map/pallas_call | solution.py:137
  27.2 3.5 fusion.7
  30.6 0.2 slice.20
  30.9 2.0 convolution_multiply_fusion
  32.9 1.3 convolution_bitcast_fusion
  34.1 0.6 fusion
  34.7 0.3 copy.8
  35.0 0.2 mul.73
  35.3 12.6 %shard_map.69 = f32[32,32,256]{2,1,0:T(8,128)S(1)} custom-call(f32[32,256]{1,0:T(8,128)S(1)} %slice.24.x_ref), custom_call_target="tpu_custom_call" | custom-call | tf_op jit(solution)/shard_map/pallas_call | solution.py:137
  47.9 1.8 convolution_bitcast_fusion.3.k_ref
  49.8 7.9 %shard_map.70 = f32[256,256]{1,0:T(8,128)S(1)} custom-call(f32[256,256]{1,0:T(8,128)S(1)} %convolution_bitcast_fusion.3.k_ref), custom_call_target="tpu_custom_call" | custom-call | tf_op jit(solution)/shard_map/pallas_call | solution.py:75
  57.6 1.0 fusion.15
  58.7 0.6 fusion.16.x_ref
  59.3 12.3 %shard_map.71 = f32[32,32,256]{2,1,0:T(8,128)S(1)} custom-call(f32[32,256]{1,0:T(8,128)S(1)} %fusion.16.x_ref), custom_call_target="tpu_custom_call" | custom-call | tf_op jit(solution)/shard_map/pallas_call | solution.py:137
  71.6 1.8 convolution_bitcast_fusion.2.k_ref
  73.5 7.9 %shard_map.72 = f32[256,256]{1,0:T(8,128)S(1)} custom-call(f32[256,256]{1,0:T(8,128)S(1)} %convolution_bitcast_fusion.2.k_ref), custom_call_target="tpu_custom_call" | custom-call | tf_op jit(solution)/shard_map/pallas_call | solution.py:75
  81.3 1.0 fusion.17
  82.3 0.6 fusion.18.x_ref
  82.9 12.2 %shard_map.73 = f32[32,32,256]{2,1,0:T(8,128)S(1)} custom-call(f32[32,256]{1,0:T(8,128)S(1)} %fusion.18.x_ref), custom_call_target="tpu_custom_call" | custom-call | tf_op jit(solution)/shard_map/pallas_call | solution.py:137
  95.1 1.8 convolution_bitcast_fusion.1.k_ref
  96.9 7.9 %shard_map.74 = f32[256,256]{1,0:T(8,128)S(1)} custom-call(f32[256,256]{1,0:T(8,128)S(1)} %convolution_bitcast_fusion.1.k_ref), custom_call_target="tpu_custom_call" | custom-call | tf_op jit(solution)/shard_map/pallas_call | solution.py:75
  104.8 2.0 fusion.19
  106.8 1.2 slice-done
  108.0 0.1 fusion.3
  108.1 0.5 broadcast_multiply_fusion
  108.6 4.6 %fusion.11 = f32[32,64,128]{2,1,0:T(8,128)} fusion(f32[32,64,128]{2,1,0:T(8,128)S(1)} %bitcast.92, f32[32,200,128]{2,1,0:T(8,128)} %copy-done.1), kind=kOutput, calls=%fused_computation.30 | convolution fusion | flops 402653184 | bytes 4194304 | tf_op jit(solution)/shard_map/dot_general | solution.py:230
  113.2 2.5 reshape.62
  115.7 3.6 broadcast_select_fusion
  119.3 22.8 %shard_map.75 = f32[256,256]{1,0:T(8,128)S(1)} custom-call(f32[256,256]{1,0:T(8,128)S(1)} %get-tuple-element.6.u_ref), custom_call_target="tpu_custom_call" | custom-call | tf_op jit(solution)/shard_map/pallas_call | solution.py:178
  142.1 0.4 fusion.20.u_ref
  142.5 17.8 %shard_map.76 = f32[256,256]{1,0:T(8,128)S(1)} custom-call(f32[256,256]{1,0:T(8,128)S(1)} %fusion.20.u_ref), custom_call_target="tpu_custom_call" | custom-call | tf_op jit(solution)/shard_map/pallas_call | solution.py:178
  160.3 0.6 fusion.22.u_ref
  160.9 18.5 %shard_map.78.k_ref = f32[256,256]{1,0:T(8,128)S(1)} custom-call(f32[256,256]{1,0:T(8,128)S(1)} %fusion.22.u_ref), custom_call_target="tpu_custom_call" | custom-call | tf_op jit(solution)/shard_map/pallas_call | solution.py:178
  179.4 7.9 %shard_map.79 = f32[256,256]{1,0:T(8,128)S(1)} custom-call(f32[256,256]{1,0:T(8,128)S(1)} %shard_map.78.k_ref), custom_call_target="tpu_custom_call" | custom-call | tf_op jit(solution)/shard_map/pallas_call | solution.py:75
  187.2 0.6 fusion.21.u_ref
  187.8 18.9 %shard_map.77 = f32[256,256]{1,0:T(8,128)S(1)} custom-call(f32[256,256]{1,0:T(8,128)S(1)} %fusion.21.u_ref), custom_call_target="tpu_custom_call" | custom-call | tf_op jit(solution)/shard_map/pallas_call | solution.py:178
  206.7 0.4 fusion.23
  207.2 0.4 fusion.24.u_ref
  207.5 18.7 %shard_map.80 = f32[256,256]{1,0:T(8,128)S(1)} custom-call(f32[256,256]{1,0:T(8,128)S(1)} %fusion.24.u_ref), custom_call_target="tpu_custom_call" | custom-call | tf_op jit(solution)/shard_map/pallas_call | solution.py:178
  226.2 0.6 fusion.26.u_ref
  226.8 19.2 %shard_map.82.k_ref = f32[256,256]{1,0:T(8,128)S(1)} custom-call(f32[256,256]{1,0:T(8,128)S(1)} %fusion.26.u_ref), custom_call_target="tpu_custom_call" | custom-call | tf_op jit(solution)/shard_map/pallas_call | solution.py:178
  246.1 7.9 %shard_map.83 = f32[256,256]{1,0:T(8,128)S(1)} custom-call(f32[256,256]{1,0:T(8,128)S(1)} %shard_map.82.k_ref), custom_call_target="tpu_custom_call" | custom-call | tf_op jit(solution)/shard_map/pallas_call | solution.py:75
  253.9 0.6 fusion.25.u_ref
  254.5 16.1 %shard_map.81 = f32[256,256]{1,0:T(8,128)S(1)} custom-call(f32[256,256]{1,0:T(8,128)S(1)} %fusion.25.u_ref), custom_call_target="tpu_custom_call" | custom-call | tf_op jit(solution)/shard_map/pallas_call | solution.py:178
  270.6 0.4 fusion.27
  271.0 0.4 fusion.28.u_ref
  271.4 21.4 %shard_map.84 = f32[256,256]{1,0:T(8,128)S(1)} custom-call(f32[256,256]{1,0:T(8,128)S(1)} %fusion.28.u_ref), custom_call_target="tpu_custom_call" | custom-call | tf_op jit(solution)/shard_map/pallas_call | solution.py:178
  292.8 0.6 fusion.30.u_ref
  293.4 18.5 %shard_map.86.k_ref = f32[256,256]{1,0:T(8,128)S(1)} custom-call(f32[256,256]{1,0:T(8,128)S(1)} %fusion.30.u_ref), custom_call_target="tpu_custom_call" | custom-call | tf_op jit(solution)/shard_map/pallas_call | solution.py:178
  311.8 7.9 %shard_map.87 = f32[256,256]{1,0:T(8,128)S(1)} custom-call(f32[256,256]{1,0:T(8,128)S(1)} %shard_map.86.k_ref), custom_call_target="tpu_custom_call" | custom-call | tf_op jit(solution)/shard_map/pallas_call | solution.py:75
  319.7 0.6 fusion.29.u_ref
  320.3 19.3 %shard_map.85 = f32[256,256]{1,0:T(8,128)S(1)} custom-call(f32[256,256]{1,0:T(8,128)S(1)} %fusion.29.u_ref), custom_call_target="tpu_custom_call" | custom-call | tf_op jit(solution)/shard_map/pallas_call | solution.py:178
  339.6 0.4 multiply_reduce_fusion
  340.0 2.5 dot_general.92
  342.5 2.2 fusion.4
  344.8 0.1 pad_maximum_fusion
  344.9 25.6 %shard_map.88 = f32[40,256]{1,0:T(8,128)S(1)} custom-call(f32[1280,256]{1,0:T(8,128)S(1)} %bitcast.86), custom_call_target="tpu_custom_call" | custom-call | tf_op jit(solution)/shard_map/pallas_call | solution.py:208
  370.6 0.8 copy.9
  371.4 0.6 slice_multiply_fusion
  (17 shorter events, 0.1 us)
Async XLA Ops:
  0.6 1.8 copy-start
  0.6 4.5 %copy-start.2 = (bf16[128,4096]{1,0:T(8,128)(2,1)S(1)}, bf16[128,4096]{1,0:T(8,128)(2,1)}, u32[]{:S(2)}) copy-start(bf16[128,4096]{1,0:T(8,128)(2,1)} %param.6) | copy-start | bytes 3145732
  0.7 4.5 %copy-start.3 = (bf16[64,4096]{1,0:T(8,128)(2,1)S(1)}, bf16[64,4096]{1,0:T(8,128)(2,1)}, u32[]{:S(2)}) copy-start(bf16[64,4096]{1,0:T(8,128)(2,1)} %param.9) | copy-start | bytes 1572868
  2.4 3.2 copy-start.4
  27.1 7.0 %copy-start.1 = (f32[32,200,128]{2,1,0:T(8,128)}, f32[32,200,128]{2,1,0:T(8,128)S(1)}, u32[]{:S(2)}) copy-start(f32[32,200,128]{2,1,0:T(8,128)S(1)} %shard_map.68) | copy-start | bytes 9830404
  106.8 1.2 slice-start

commit v2 on v0

v2 whole, which is shorter than its diff:
```python
import functools
import math

import jax
import jax.numpy as jnp
from jax import lax
from jax.experimental import pallas as pl
from jax.experimental.pallas import tpu as pltpu
from jax.sharding import PartitionSpec as P

RANK = 256
ITERS = 2
DOC_DEV = 32
F32 = jnp.float32
BF = jnp.bfloat16
MESH = pl.DeviceIdType.MESH
VM = pl.BlockSpec(memory_space=pltpu.VMEM)
HI = lax.Precision.HIGHEST
SPAN = 600.0


def split3(x):
    h=x.astype(BF); r=x-h.astype(F32); m=r.astype(BF); l=(r-m.astype(F32)).astype(BF)
    return h,m,l

def panel_factor(P, p, nb):
    n=P.shape[1]
    lane=lax.broadcasted_iota(jnp.int32,(nb,n),1)
    row=lax.broadcasted_iota(jnp.int32,(nb,n),0)
    rowb=lax.broadcasted_iota(jnp.int32,(nb,128),0)
    S=jnp.ones((nb,128),F32)
    for leaf in range(nb//8):
        c0=nb*p+8*leaf
        B=[jnp.broadcast_to(P[:,c0+j:c0+j+1],(nb,128)) for j in range(8)]
        for k in range(8):
            rk=8*leaf+k
            pv=B[k][rk:rk+1,:]
            rp=1.0/pv
            f=jnp.where(rowb>rk,B[k]*rp,0.0)
            for j in range(k+1,8):
                B[j]=B[j]-f*B[j][rk:rk+1,:]
            S=jnp.where(rowb==rk,lax.rsqrt(pv),S)
            hit=lane==(c0+k)
            prow=jnp.where(hit[0:1],1.0,P[rk:rk+1,:])
            ff=jnp.concatenate([f]*(n//128),axis=1)
            P=jnp.where(hit&(row>rk),0.0,jnp.where(hit&(row==rk),1.0,P))-ff*prow
    return P*jnp.concatenate([S]*(n//128),axis=1)

def chol_inv_body(A, first, last, nb=32):
    n=A.shape[0]
    for p in range(first, last):
        r0=nb*p; r1=r0+nb
        R=panel_factor(A[r0:r1,:],p,nb)
        A[r0:r1,:]=R
        if r1<n:
            plane=lax.broadcasted_iota(jnp.int32,(nb,n),1); prow=lax.broadcasted_iota(jnp.int32,(nb,n),0)
            R=jnp.where((plane>=r0)&(plane<r1)&(plane-r0>prow),0.0,R)
            h,m,l=split3(R)
            rhs=jnp.concatenate([h,m,h,l,m,h],axis=0)
            lh,lm,ll=h[:,r1:],m[:,r1:],l[:,r1:]
            lhs=jnp.concatenate([lh,lh,lm,lh,lm,ll],axis=0)
            upd=lax.dot_general(lhs,rhs,(((0,),(0,)),((),())),preferred_element_type=F32)
            lane=lax.broadcasted_iota(jnp.int32,(n-r1,n),1)
            T=A[r1:,:]
            A[r1:,:]=jnp.where((lane>=r0)&(lane<r1),0.0,T)-upd


def chol_kernel(k_ref, w_ref, A):
    A[...] = k_ref[...]
    chol_inv_body(A, 0, 8)
    r = lax.broadcasted_iota(jnp.int32, (256, 256), 0); c = lax.broadcasted_iota(jnp.int32, (256, 256), 1)
    w_ref[...] = jnp.where(c <= r, A[...], 0.0)


def chol_inv(K):
    return pl.pallas_call(
        chol_kernel, out_shape=jax.ShapeDtypeStruct((256, 256), F32), in_specs=[VM], out_specs=VM,
        scratch_shapes=[pltpu.VMEM((256, 256), F32)], compiler_params=pltpu.CompilerParams(vmem_limit_bytes=32 << 20),
    )(K)


def rcopy(src, dst, ss, rs, dev):
    return pltpu.make_async_remote_copy(src_ref=src, dst_ref=dst, send_sem=ss, recv_sem=rs, device_id=dev, device_id_type=MESH)


def mm(a, b, ca=1, cb=0):
    return lax.dot_general(a, b, (((ca,), (cb,)), ((), ())), precision=HI, preferred_element_type=F32)


def dotb(a, b, ca=1, cb=0):
    return lax.dot_general(a, b, (((ca,), (cb,)), ((), ())), preferred_element_type=F32)


def ds8(i, r):
    return pl.ds(pl.multiple_of(i * r, 8), r)


class Axis:
    def __init__(self, n, me, dev, sent):
        self.n, self.me, self.dev, self.sent = n, me, dev, sent

    def send(self, src, dst, ss, rs, q):
        c = rcopy(src, dst, ss, rs, self.dev(q))
        c.start()
        self.sent.append(c)

    def each(self, f):
        for k in range(1, self.n):
            f(k, lax.rem(self.me + k, self.n))

    def scatter(self, src, buf, ss, rs):
        n, r = self.n, src.shape[0] // self.n
        self.each(lambda k, q: self.send(src.at[ds8(q, r)], buf.at[n - k], ss.at[k], rs.at[n - k], q))

    def gather_sum(self, src, buf, ss, rs):
        r = src.shape[0] // self.n
        acc = src[ds8(self.me, r), :]
        for k in range(1, self.n):
            rcopy(buf.at[k], buf.at[k], ss.at[k], rs.at[k], self.dev(self.me)).wait_recv()
            acc = acc + buf[k]
        return acc

    def spread(self, src, out, r, ss, rs):
        n = self.n
        self.each(lambda k, q: self.send(src, out.at[ds8(self.me, r)], ss.at[k], rs.at[n - k], q))

    def collect(self, out, r, ss, rs):
        self.each(lambda k, q: rcopy(out.at[ds8(q, r)], out.at[ds8(q, r)], ss.at[k], rs.at[k], self.dev(self.me)).wait_recv())


def ag_dev(g, me, x_ref, out, ss, rs, ls):
    core = lax.rem(me, 2); x = lax.rem(me // 2, 4); y = me // 8
    hr = x_ref.shape[0] // 2
    def did(yy, xx): return (g, (yy * 4 + xx) * 2 + core)
    def slot(yy, xx): return core * 16 + yy * 4 + xx
    xs = [lax.rem(x + k, 4) for k in (1, 2, 3)]; ys = [lax.rem(y + k, 4) for k in (1, 2, 3)]
    sib = (g, (y * 4 + x) * 2 + 1 - core)
    mine = slot(y, x)
    lc = pltpu.make_async_copy(x_ref, out.at[mine], ls); lc.start()
    H = [pl.ds(0, hr), pl.ds(hr, hr)]
    sends = []
    def send(src, owner, h, dev):
        c = rcopy(src, out.at[owner, H[h]], ss.at[len(sends)], rs.at[owner, h], dev); c.start(); sends.append(c)
    for k in range(3):
        send(x_ref.at[H[0]], mine, 0, did(y, xs[k]))
        send(x_ref.at[H[1]], mine, 1, did(ys[k], x))
    for k in range(3):
        send(x_ref.at[H[0]], mine, 0, did(ys[k], x))
        send(x_ref.at[H[1]], mine, 1, did(y, xs[k]))
    for h in range(2): send(x_ref.at[H[h]], mine, h, sib)
    def wait(owner, h):
        rcopy(out.at[owner, H[h]], out.at[owner, H[h]], ss.at[0], rs.at[owner, h], sib).wait_recv()
    order = (0, 2, 1)
    for k in order:
        ox = slot(y, xs[k]); oy = slot(ys[k], x)
        wait(ox, 0)
        for q in range(3): send(out.at[ox, H[0]], ox, 0, did(ys[q], x))
        send(out.at[ox, H[0]], ox, 0, sib)
        wait(oy, 1)
        for q in range(3): send(out.at[oy, H[1]], oy, 1, did(y, xs[q]))
        send(out.at[oy, H[1]], oy, 1, sib)
    for k in order:
        ox = slot(y, xs[k]); oy = slot(ys[k], x)
        wait(oy, 0); send(out.at[oy, H[0]], oy, 0, sib)
        wait(ox, 1); send(out.at[ox, H[1]], ox, 1, sib)
    for k in order:
        for q in order:
            o = slot(ys[k], xs[q])
            for h in range(2):
                wait(o, h); send(out.at[o, H[h]], o, h, sib)
    lc.wait()
    def rest(j, c):
        for h in range(2): wait((1 - core) * 16 + j, h)
        return c
    lax.fori_loop(0, 16, rest, 0)
    for c in sends: c.wait_send()


def token_blocks(hs_parts, gt_cat, own3, idx, tokall, b0):
    Hs, Gc = [], []
    for s in range(4):
        Hs.append(split3(tokall[b0 + s, 0:128, :]))
        h, m, l = split3(tokall[b0 + s, 128:192, :])
        Gc.append(jnp.concatenate([h, m, h, l, m, h], axis=0))
    h, m, l = [jnp.concatenate([x[i] for x in Hs], axis=0) for i in range(3)]
    ah, am, al = hs_parts
    A = dotb(jnp.concatenate([ah, am], axis=1), jnp.concatenate([h, h], axis=1), 1, 1)
    A = A + dotb(jnp.concatenate([ah, al], axis=1), jnp.concatenate([m, h], axis=1), 1, 1)
    A = A + dotb(jnp.concatenate([ah, am], axis=1), jnp.concatenate([l, m], axis=1), 1, 1)
    B = dotb(gt_cat, jnp.concatenate(Gc, axis=1))
    th, tm, tl = split3(A * B)
    T = dotb(own3, jnp.concatenate([th, tm, tl], axis=0))
    r4 = lax.broadcasted_iota(jnp.int32, (128, 512), 0).astype(F32)
    marks = jnp.concatenate([tokall[b0 + s, 192:193, :] for s in range(4)], axis=1)
    O4 = (r4 == marks).astype(F32)
    O4b = O4.astype(BF)
    th, tm, tl = split3(T)
    G4 = dotb(th, O4b, 1, 1) + dotb(tm, O4b, 1, 1) + dotb(tl, O4b, 1, 1)
    return G4, O4, Hs


def merge_kernel(hs_in, gt_in, idx_in, coef, basis, state, tok, tokall, M, Gown, ysrc, Y, A, S, X, Z, W0, W0S, UP, SB, HB, UB, U, VP, VB, V, KP, KB, K,
                 CF, CSB, CHB, CB, SQ, SQB, ag_s, ag_r, ag_l, bs, us, ur, us2, ur2, vs, vr, vs2, vr2, ks, kr, ks2, kr2, cs, cr, qs, qr, zs, zr):
    g = lax.axis_index("group"); d = lax.axis_index("dev")
    core = lax.rem(d, 2); p = d // 2
    sib = (g, 2 * p + 1 - core)
    sent = []
    def drain():
        @pl.when(g == 0)
        def _():
            for k in range(1, 8):
                rcopy(Z.at[ds8(0, 32)], Z.at[ds8(0, 32)], zs.at[k], zr.at[0], (g, d)).wait_send()
                rcopy(Z.at[ds8(0, 32)], Z.at[ds8(0, 32)], zs.at[16 + k], zr.at[0], (g, d)).wait_send()
        for c in sent:
            c.wait_send()
    AC = Axis(16, p, lambda i: (g, 2 * i + core), sent)
    AG = Axis(8, g, lambda i: (i, d), sent)
    b = pltpu.get_barrier_semaphore()
    AC.each(lambda k, q: pl.semaphore_signal(b, inc=1, device_id=AC.dev(q), device_id_type=MESH))
    AG.each(lambda k, q: pl.semaphore_signal(b, inc=1, device_id=AG.dev(q), device_id_type=MESH))
    pl.semaphore_signal(b, inc=1, device_id=sib, device_id_type=MESH)
    tok[0:128, :] = hs_in[...]
    tok[128:192, :] = gt_in[...]
    idx = idx_in[0:1, :]
    tok[192:200, :] = jnp.broadcast_to(idx + 32 * lax.rem(p, 4), (8, 128)).astype(F32)
    half = lambda c, n: pl.ds(pl.multiple_of(c * n, 8), n)
    pl.semaphore_wait(b, 23)
    ag_dev(g, d, tok, tokall, ag_s.at[0], ag_r.at[0], ag_l.at[0])
    hs_parts = split3(tok[0:128, :])
    h, m, l = split3(tok[128:192, :].T)
    gt_cat = jnp.concatenate([h, h, m, h, m, l], axis=1)
    drow = lax.broadcasted_iota(jnp.int32, (32, 128), 0)
    own = (jnp.broadcast_to(idx, (32, 128)) == drow).astype(BF)
    own3 = jnp.concatenate([own, own, own], axis=1)
    par = lax.rem(d, 4)
    gbase = pl.multiple_of((d // 4) * 8, 8)
    r8 = lax.broadcasted_iota(jnp.int32, (8, 128), 0)
    def four(q, c):
        G4, O4, Hs = token_blocks(hs_parts, gt_cat, own3, idx, tokall, 4 * q)
        Gown[q] = G4 * (1.0 / 8192)
        for s in range(4):
            g8 = tokall[4 * q + s, pl.ds(128 + gbase, 8), :]
            O1 = O4[32 * s:32 * s + 32, 128 * s:128 * s + 128]
            g0 = jnp.sum(jnp.where(r8 == 2 * par, g8, 0.0), axis=0, keepdims=True)
            g1 = jnp.sum(jnp.where(r8 == 2 * par + 1, g8, 0.0), axis=0, keepdims=True)
            wh, wm, wl = split3(jnp.concatenate([O1 * g0, O1 * g1], axis=0))
            h, m, l = Hs[s]
            mr = dotb(jnp.concatenate([wh, wh, wm, wh, wm, wl], axis=1), jnp.concatenate([h, m, h, l, m, h], axis=0)) * (1.0 / math.sqrt(8192))
            M[ds8(4 * q + s, 32), 0:128] = mr[0:32]
            M[ds8(4 * q + s, 32), 128:256] = mr[32:64]
        return c
    lax.fori_loop(0, 8, four, 0)
    y0, y1 = Gown[0], Gown[4]
    ysrc[0] = jnp.concatenate([(y1 if s % 2 else y0)[:, 32 * (s // 2):32 * (s // 2) + 32] for s in range(8)], axis=1)
    for it in range(3):
        ag_dev(g, d, ysrc.at[it], Y.at[it], ag_s.at[it + 1], ag_r.at[it + 1], ag_l.at[it + 1])
        if it < 2:
            acc = jnp.zeros((32, 256), F32)
            for q in range(8):
                acc = acc + mm(Gown[q], Y[it, 4 * q:4 * q + 4, :, :].reshape(128, 256))
            ysrc[it + 1] = acc
    def zpart(q, acc):
        yb = Y[2, pl.ds(8 * q, 8), :, :].reshape(256, 256)
        return acc + mm(yb, M[ds8(q, 256), :], 0, 0)
    def gram(q, acc):
        yb = Y[2, pl.ds(8 * q, 8), :, :].reshape(256, 256)
        return acc + mm(yb, yb, 0, 0)
    zero = jnp.zeros((256, 256), F32)
    z1 = lax.fori_loop(0, 4, zpart, zero)
    Z[...] = z1
    @pl.when(g == 0)
    def _():
        for k in range(1, 8):
            rcopy(Z.at[ds8(k, 32)], X.at[ds8(k, 32)], zs.at[k], zr.at[0], (k, d)).start()
        X[0:32, :] = Z[0:32, :]
    A[...] = lax.fori_loop(0, 4, gram, zero)
    chol_inv_body(A, 0, 3)
    @pl.when(g > 0)
    def _():
        rcopy(X.at[ds8(g, 32)], X.at[ds8(g, 32)], zs.at[0], zr.at[0], (g, d)).wait_recv()
    AG.spread(X.at[ds8(g, 32)], X, 32, zs.at[pl.ds(8, 8)], zr.at[pl.ds(8, 8)])
    chol_inv_body(A, 3, 8)
    row = lax.broadcasted_iota(jnp.int32, (256, 256), 0); col = lax.broadcasted_iota(jnp.int32, (256, 256), 1)
    tri = col <= row
    diag = jnp.sum(jnp.where(col == row, A[...], 0.0), axis=0, keepdims=True)
    hi = jnp.max(diag, axis=1, keepdims=True); lo = jnp.min(diag, axis=1, keepdims=True)
    W = jnp.where(tri, A[...], 0.0) + jnp.where(hi < SPAN * lo, 0.0, jnp.nan)
    W0S[...] = W
    @pl.when(g == 0)
    def _():
        for k in range(1, 8):
            rcopy(W0S.at[ds8(k, 32)], W0.at[ds8(k, 32)], zs.at[16 + k], zr.at[16], (k, d)).start()
        W0[0:32, :] = W0S[0:32, :]
    S[...] = mm(W, z1)
    AG.collect(X, 32, zs.at[pl.ds(8, 8)], zr.at[pl.ds(8, 8)])
    xt = X[...].T
    for it in range(3):
        UP[it] = mm(S[...], xt)
        to_sib = rcopy(UP.at[it, half(1 - core, 128)], SB.at[it], bs.at[2 * it], bs.at[8 + 2 * it], sib)
        to_sib.start()
        sent.append(to_sib)
        if it == 0:
            @pl.when(g > 0)
            def _():
                rcopy(W0.at[ds8(g, 32)], W0.at[ds8(g, 32)], zs.at[0], zr.at[16], (g, d)).wait_recv()
            AG.spread(W0.at[ds8(g, 32)], W0, 32, zs.at[pl.ds(24, 8)], zr.at[pl.ds(24, 8)])
        to_sib.wait_recv()
        HB[it] = UP[it, half(core, 128), :] + SB[it]
        AC.scatter(HB.at[it], UB.at[it], us.at[it], ur.at[it])
        uh = U.at[it, half(core, 128)]
        uh[ds8(p, 8), :] = AC.gather_sum(HB.at[it], UB.at[it], us.at[it], ur.at[it])
        AC.spread(uh.at[ds8(p, 8)], uh, 8, us2.at[it], ur2.at[it])
        AC.collect(uh, 8, us2.at[it], ur2.at[it])
        swap = rcopy(uh, uh, bs.at[2 * it + 1], bs.at[9 + 2 * it], sib)
        swap.start()
        sent.append(swap)
        swap.wait_recv()
        u = U[it]
        if it == 2:
            mine = core * 16 + p
            KP[...] = mm(u, u, 0, 0)
            KB[ds8(g, 8), :] = KP[ds8(mine, 8), :]
            AG.spread(KP.at[ds8(mine, 8)], KB, 8, ks, kr)
        VP[it] = mm(S[...], u, 0, 0)
        AG.scatter(VP.at[it], VB.at[it], vs.at[it], vr.at[it])
        if it == 2:
            AG.collect(KB, 8, ks, kr)
            acc = KB[0:8, :]
            for q in range(1, 8):
                acc = acc + KB[8 * q:8 * q + 8, :]
            kh = K.at[half(core, 128)]
            kh[ds8(p, 8), :] = acc
            AC.spread(kh.at[ds8(p, 8)], kh, 8, ks2, kr2)
        V[it, ds8(g, 32), :] = AG.gather_sum(VP.at[it], VB.at[it], vs.at[it], vr.at[it])
        AG.spread(V.at[it, ds8(g, 32)], V.at[it], 32, vs2.at[it], vr2.at[it])
        if it == 2:
            AC.collect(kh, 8, ks2, kr2)
            swap_k = rcopy(kh, kh, bs.at[6], bs.at[14], sib)
            swap_k.start()
            sent.append(swap_k)
            swap_k.wait_recv()
            A[...] = K[...]
            chol_inv_body(A, 0, 3)
        AG.collect(V.at[it], 32, vs2.at[it], vr2.at[it])
        if it == 0:
            AG.collect(W0, 32, zs.at[pl.ds(24, 8)], zr.at[pl.ds(24, 8)])
            xt = mm(V[0], W0[...], 1, 1)
        else:
            xt = V[it]
    def cpart(q, c):
        CF[ds8(q, 256), :] = mm(M[ds8(q, 256), :], V[2])
        return c
    lax.fori_loop(0, 4, cpart, 0)
    csib = rcopy(CF.at[half(1 - core, 512)], CSB, bs.at[7], bs.at[15], sib)
    csib.start()
    sent.append(csib)
    chol_inv_body(A, 3, 5)
    csib.wait_recv()
    CHB[...] = CF[half(core, 512), :] + CSB[...]
    AC.scatter(CHB, CB, cs, cr)
    chol_inv_body(A, 5, 8)
    diag = jnp.sum(jnp.where(col == row, A[...], 0.0), axis=0, keepdims=True)
    hi = jnp.max(diag, axis=1, keepdims=True); lo = jnp.min(diag, axis=1, keepdims=True)
    state[...] = jnp.broadcast_to(jnp.where(hi < SPAN * lo, 1.0, 0.0), (8, 128))
    W = jnp.where(tri, A[...], 0.0)
    mt = mm(V[2], W, 1, 1)
    SQ[0] = jnp.broadcast_to(jnp.sum(mt * mt, axis=0, keepdims=True), (8, 256))
    qsib = rcopy(SQ.at[0], SQ.at[1], qs.at[0], qr.at[0], sib)
    qsib.start()
    sent.append(qsib)
    cfs = mm(AC.gather_sum(CHB, CB, cs, cr), W, 1, 1)
    qsib.wait_recv()
    SQB[ds8(p, 8), :] = SQ[0] + SQ[1]
    AC.spread(SQB.at[ds8(p, 8)], SQB, 8, qs, qr)
    AC.collect(SQB, 8, qs, qr)
    sq = SQB[0:8, :]
    for q in range(1, 16):
        sq = sq + SQB[8 * q:8 * q + 8, :]
    f = 1.0 / jnp.sqrt(sq[0:1, :] / 8192.0 + 1e-06)
    coef[...] = cfs * (f * (1.0 / math.sqrt(8192)))
    basis[...] = (mt * f).T
    drain()


def merge_all(hs, gt, idx):
    D = pltpu.SemaphoreType.DMA
    V = lambda *s: pltpu.VMEM(s, F32)
    return pl.pallas_call(
        merge_kernel,
        out_shape=[jax.ShapeDtypeStruct((32, 256), F32), jax.ShapeDtypeStruct((256, 256), F32), jax.ShapeDtypeStruct((8, 128), F32)],
        in_specs=[VM, VM, VM], out_specs=[VM, VM, VM],
        scratch_shapes=[
            V(200, 128), V(32, 200, 128), V(1024, 256), V(8, 32, 128), V(3, 32, 256), V(3, 32, 32, 256),
            V(256, 256), V(256, 256), V(256, 256), V(256, 256), V(256, 256), V(256, 256),
            V(3, 256, 256), V(3, 128, 256), V(3, 128, 256), V(3, 16, 8, 256), V(3, 256, 256), V(3, 256, 256), V(3, 8, 32, 256), V(3, 256, 256),
            V(256, 256), V(64, 256), V(256, 256), V(1024, 256), V(512, 256), V(512, 256), V(16, 32, 256), V(2, 8, 256), V(128, 256),
            D((4, 80)), D((4, 32, 2)), D((4,)), D((16,)),
            D((3, 16)), D((3, 16)), D((3, 16)), D((3, 16)), D((3, 8)), D((3, 8)), D((3, 8)), D((3, 8)),
            D((8,)), D((8,)), D((16,)), D((16,)), D((16,)), D((16,)), D((16,)), D((16,)), D((32,)), D((32,)),
        ],
        compiler_params=pltpu.CompilerParams(collective_id=1, has_side_effects=True, vmem_limit_bytes=56 << 20),
    )(hs, gt, idx)


def merge_slow(hs, gt, doc_index):
    def orth(Y):
        return mm(Y, chol_inv(mm(Y, Y, 0, 0)), 1, 1)
    def sum_parts(x, axis, n):
        r = x.shape[0] // n
        return lax.all_to_all(x, axis, split_axis=0, concat_axis=0, tiled=True).reshape(n, r, x.shape[1]).sum(axis=0)
    def gather(x, axis, n):
        return lax.all_to_all(jnp.tile(x, (n, 1)), axis, split_axis=0, concat_axis=0, tiled=True)
    def total(x):
        return gather(sum_parts(x, "dev", 32), "dev", 32)
    own = (doc_index == jnp.arange(DOC_DEV, dtype=jnp.int32)[:, None]).astype(F32)
    weighted = own[:, None, :] * gt[None, :, :]
    rows = mm(weighted.reshape(-1, 128), hs).reshape(DOC_DEV, 8192) * (1.0 / math.sqrt(8192))
    block = lax.all_to_all(rows, "dev", split_axis=1, concat_axis=0, tiled=True)
    G = total(mm(block, block, 1, 1))
    Q = orth(G[:, :RANK])
    for _ in range(ITERS):
        Q = orth(mm(G, Q))
    stacked = gather(mm(Q, block, 0, 0), "group", 8)
    Q = orth(total(mm(stacked, stacked[:RANK], 1, 1)))
    for _ in range(ITERS):
        Q = orth(total(mm(stacked, mm(stacked, Q, 0, 0))))
    merged = mm(Q, stacked, 0, 0)
    squares = total(jnp.broadcast_to(jnp.sum(merged * merged, axis=1)[None, :], (32, RANK)))[0]
    basis = merged * (1.0 / jnp.sqrt(squares / 8192.0 + 1e-06))[:, None]
    summed = sum_parts(mm(block, basis, 1, 1), "dev", 32)
    return summed / math.sqrt(8192), basis


def on_device(hidden_acts, out_grads, doc_index, proj_hidden, proj_grad):
    hs = lax.dot_general(hidden_acts, proj_hidden, (((1,), (1,)), ((), ())), preferred_element_type=F32)
    gt = lax.dot_general(proj_grad, out_grads, (((1,), (1,)), ((), ())), preferred_element_type=F32)
    coef, basis, state = merge_all(hs, gt, doc_index)
    return lax.cond(state[0, 0] > 0.5, lambda: (coef, basis), lambda: merge_slow(hs, gt, doc_index))


def solution(mesh):
    return jax.shard_map(
        on_device,
        mesh=mesh,
        in_specs=(
            P(("group", "dev"), None),
            P(("group", "dev"), None),
            P(("group", "dev"), None),
            P(),
            P(),
        ),
        out_specs=(P(("group", "dev"), None), P(None, "dev")),
        check_vma=False,
    )
```

time: 1250 us -> 775 us (0.62)
  waiting for transfers between devices: 652 us -> 16.5 us
  blocking collectives: 87.8 us -> 416 us
  other arithmetic: 329 us -> 7.86 us
  Pallas kernels: 0 us -> 251 us
  matrix products: 116 us -> 62.3 us
  local copies, waits for them, and re-layouts: 37.1 us -> 7.11 us
  between operations: 23.1 us -> 1.53 us
    all_to_all x1 -> x12, blocking collectives: 25.6 us -> 416 us  [the longest x6 217 us: gather(): lax.all_to_all(jnp.tile(x, (n, 1)), axis, split_axis=0, concat_axis=0, ti...]
    reduce_scatter x4 -> x0, waiting for transfers between devices: 337 us -> none  [the longest x3 255 us: merged_apply(): lax.psum_scatter(matmul(stacked, factor), 'dev', scatter_dimension=0, til...]
    another operation x54 -> x0, other arithmetic: 326 us -> none  [the longest x41 208 us: orthonormal(): lower_factor = jnp.linalg.cholesky(inner_gram)]
    pallas_call x0 -> x7, Pallas kernels: none -> 251 us  [the longest x1 204 us: merge_all(): pl.pallas_call(merge_kernel, out_shape=[jax.ShapeDtypeStruct((32, 256), F...]
    all_gather x4 -> x0, waiting for transfers between devices: 195 us -> none  [the longest x3 158 us: merged_apply(): return lax.all_gather(owned_rows, 'dev', axis=0, tiled=True)]
    psum x1 -> x0, waiting for transfers between devices: 121 us -> none  [on_device(): summed_gram = lax.psum(matmul(column_block, column_block.T), 'dev')]
    psum x1 -> x0, blocking collectives: 62.3 us -> none  [on_device(): squares = lax.psum(jnp.sum(merged * merged, axis=1), 'dev')]
    another operation x30 -> x0, matrix products: 42.1 us -> none  [the longest x18 29.2 us: orthonormal(): lax.linalg.triangular_solve(lower_factor, images, left_side=False, lower=...]
  transfers between devices with their start and end apart: 9 -> 1, of which waited for: 9 -> 1; matrix products, arithmetic and copies ran while one was open for 0% -> 0% of each run, Pallas kernels for 0% -> 0%
where the time goes in v2:
time: 775 us; the launch traced here: 767 us
  blocking collectives  416 us (54%)
  Pallas kernels  251 us (32%)
  matrix products  62.3 us (8%)
  waiting for transfers between devices  16.5 us (2%)
  other arithmetic  7.86 us (1%)
    all_to_all x6, blocking collectives, gather(): lax.all_to_all(jnp.tile(x, (n, 1)), axis, split_axis=0, concat_axis=0, ti...  217 us
    pallas_call x1, Pallas kernels, merge_all(): pl.pallas_call(merge_kernel, out_shape=[jax.ShapeDtypeStruct((32, 256), F...  204 us
    all_to_all x5, blocking collectives, sum_parts(): lax.all_to_all(x, axis, split_axis=0, concat_axis=0, tiled=True)  164 us
    dot_general x24, matrix products, mm(): lax.dot_general(a, b, (((ca,), (cb,)), ((), ())), precision=HI, preferred...  57.6 us
    pallas_call x6, Pallas kernels, chol_inv(): pl.pallas_call(chol_kernel, out_shape=jax.ShapeDtypeStruct((256, 256), F3...  47.3 us
    all_to_all x1, blocking collectives, merge_slow(): block = lax.all_to_all(rows, 'dev', split_axis=1, concat_axis=0, tiled=True)  35 us
    all_to_all x1, waiting for transfers between devices, sum_parts(): lax.all_to_all(x, axis, split_axis=0, concat_axis=0, tiled=True)  16.5 us
  transfers between devices with their start and end apart: 1, of which 1 were waited for; matrix products, arithmetic and copies ran while one was open for 0% of the time, Pallas kernels for 0%

profile of v2, /device:TPU:1, one launch (start us, length us, event | category | flops | bytes accessed | tf_op | source)
XLA Modules:
  0.0 767.2 jit_solution(8338383016978898688)
XLA Ops:
  0.6 2.0 fusion.26.gt_in
  2.7 0.2 copy-done
  2.9 2.7 fusion.25.hs_in
  5.6 204.2 %shard_map.70 = (f32[32,256]{1,0:T(8,128)S(1)}, f32[256,256]{1,0:T(8,128)}, f32[8,128]{1,0:T(8,128)}) custom-call(f32[128,128]{1,0:T(8,128)S(1)} %fusion.25.hs_in, f32[64,128]{1,0:T(8,128)S(1)} %fusion.26.gt_in, s32[1,128]{1,0:T(1,128)S(1)} %copy-done.2), custom_call_target="tpu_custom_call" | custom-call | tf_op jit(solution)/shard_map/pallas_call | solution.py:388
  209.8 1.2 slice.16
  211.7 552.8 %conditional.1 = ((f32[32,256]{1,0:T(8,128)S(1)}, f32[256,256]{1,0:T(8,128)})) conditional(s32[]{:T(128)} %bitcast.20, (s32[1,128]{1,0:T(1,128)S(1)}, f32[64,128]{1,0:T(8,128)S(1)}, f32[128,128]{1,0:T(8,128)S(1)}) %tuple.33, (f32[32,256]{1,0:T(8,128)S(1)}, f32[256,256]{1,0:T(8,128)}) %tuple.15), branch_computations={%region_0.0_spmd, %region_8.0_spmd} | conditional | flops 35839672320 | bytes 167059008 | solution.py:438
  211.8 1.0 convolution_multiply_fusion
  212.8 0.3 mul.31
  213.1 0.6 copy.17
  213.7 35.0 %all_to_all.83 = f32[32,32,256]{2,0,1:T(8,128)S(1)} all-to-all(f32[32,32,256]{2,0,1:T(8,128)S(1)} %copy.17), channel_id=1, replica_groups=mesh['group'=8,'dev'=32] {'dev'}, dimensions={1} | all-to-all | bytes 2097152 | tf_op jit(solution)/shard_map/cond/branch_0_fun/all_to_all | solution.py:418
  248.7 3.8 fusion
  252.5 54.7 %all_to_all.84 = f32[32,32,1024]{2,1,0:T(8,128)} all-to-all(f32[32,32,1024]{2,1,0:T(8,128)S(1)} %fusion), channel_id=1, replica_groups=mesh['group'=8,'dev'=32] {'dev'}, dimensions={0} | all-to-all | bytes 8388608 | tf_op jit(solution)/shard_map/cond/branch_0_fun/all_to_all | solution.py:410
  307.3 2.4 reduce_sum.56
  309.7 0.5 tile.0
  310.2 55.2 %all_to_all.85 = f32[32,32,1024]{2,1,0:T(8,128)S(1)} all-to-all(f32[32,32,1024]{2,1,0:T(8,128)S(1)} %tile.0), channel_id=1, replica_groups=mesh['group'=8,'dev'=32] {'dev'}, dimensions={0} | all-to-all | bytes 8388608 | tf_op jit(solution)/shard_map/cond/branch_0_fun/all_to_all | solution.py:412
  365.4 1.8 fusion.6.k_ref
  367.3 7.9 %branch_0_fun.6 = f32[256,256]{1,0:T(8,128)S(1)} custom-call(f32[256,256]{1,0:T(8,128)S(1)} %fusion.6.k_ref), custom_call_target="tpu_custom_call" | custom-call | tf_op jit(solution)/shard_map/cond/branch_0_fun/pallas_call | solution.py:76
  375.2 1.0 fusion.4
  376.2 3.4 fusion.13
  379.6 2.2 fusion.14.k_ref
  381.9 7.9 %branch_0_fun.7 = f32[256,256]{1,0:T(8,128)S(1)} custom-call(f32[256,256]{1,0:T(8,128)S(1)} %fusion.14.k_ref), custom_call_target="tpu_custom_call" | custom-call | tf_op jit(solution)/shard_map/cond/branch_0_fun/pallas_call | solution.py:76
  389.7 1.0 fusion.15
  390.8 3.4 fusion.16
  394.2 1.8 fusion.17.k_ref
  396.0 8.0 %branch_0_fun.8 = f32[256,256]{1,0:T(8,128)S(1)} custom-call(f32[256,256]{1,0:T(8,128)S(1)} %fusion.17.k_ref), custom_call_target="tpu_custom_call" | custom-call | tf_op jit(solution)/shard_map/cond/branch_0_fun/pallas_call | solution.py:76
  404.1 1.0 fusion.18
  405.1 1.8 fusion.19
  406.9 0.2 tile.1
  407.1 55.5 %all_to_all.86 = f32[8,256,256]{2,1,0:T(8,128)S(1)} all-to-all(f32[8,256,256]{2,1,0:T(8,128)S(1)} %tile.1), channel_id=1, replica_groups=mesh['group'=8,'dev'=32] {'group'}, dimensions={0} | all-to-all | bytes 4194304 | tf_op jit(solution)/shard_map/cond/branch_0_fun/all_to_all | solution.py:412
  462.6 1.9 fusion.8
  464.5 33.8 %all_to_all.87 = f32[32,64,256]{2,1,0:T(8,128)} all-to-all(f32[32,64,256]{2,1,0:T(8,128)S(1)} %fusion.8), channel_id=1, replica_groups=mesh['group'=8,'dev'=32] {'dev'}, dimensions={0} | all-to-all | bytes 4194304 | tf_op jit(solution)/shard_map/cond/branch_0_fun/all_to_all | solution.py:410
  498.3 1.7 reduce_sum.57
  500.0 0.2 tile.2
  500.3 31.9 %all_to_all.88 = f32[32,64,256]{2,1,0:T(8,128)S(1)} all-to-all(f32[32,64,256]{2,1,0:T(8,128)S(1)} %tile.2), channel_id=1, replica_groups=mesh['group'=8,'dev'=32] {'dev'}, dimensions={0} | all-to-all | bytes 4194304 | tf_op jit(solution)/shard_map/cond/branch_0_fun/all_to_all | solution.py:412
  532.2 3.5 convolution_bitcast_fusion.4.k_ref
  535.7 7.9 %branch_0_fun.9 = f32[256,256]{1,0:T(8,128)S(1)} custom-call(f32[256,256]{1,0:T(8,128)S(1)} %convolution_bitcast_fusion.4.k_ref), custom_call_target="tpu_custom_call" | custom-call | tf_op jit(solution)/shard_map/cond/branch_0_fun/pallas_call | solution.py:76
  543.5 1.9 fusion.20
  545.5 3.7 convolution_bitcast_fusion.3
  549.1 1.9 fusion.21
  551.0 32.3 %all_to_all.89 = f32[32,64,256]{2,1,0:T(8,128)} all-to-all(f32[32,64,256]{2,1,0:T(8,128)S(1)} %fusion.21), channel_id=1, replica_groups=mesh['group'=8,'dev'=32] {'dev'}, dimensions={0} | all-to-all | bytes 4194304 | tf_op jit(solution)/shard_map/cond/branch_0_fun/all_to_all | solution.py:410
  583.3 1.7 reduce_sum.58
  585.0 0.2 tile.3
  585.3 31.9 %all_to_all.90 = f32[32,64,256]{2,1,0:T(8,128)S(1)} all-to-all(f32[32,64,256]{2,1,0:T(8,128)S(1)} %tile.3), channel_id=1, replica_groups=mesh['group'=8,'dev'=32] {'dev'}, dimensions={0} | all-to-all | bytes 4194304 | tf_op jit(solution)/shard_map/cond/branch_0_fun/all_to_all | solution.py:412
  617.1 3.5 convolution_bitcast_fusion.2.k_ref
  620.6 7.9 %branch_0_fun.10 = f32[256,256]{1,0:T(8,128)S(1)} custom-call(f32[256,256]{1,0:T(8,128)S(1)} %convolution_bitcast_fusion.2.k_ref), custom_call_target="tpu_custom_call" | custom-call | tf_op jit(solution)/shard_map/cond/branch_0_fun/pallas_call | solution.py:76
  628.5 1.9 fusion.22
  630.4 3.7 convolution_bitcast_fusion.1
  634.1 1.9 fusion.23
  636.0 32.3 %all_to_all.91 = f32[32,64,256]{2,1,0:T(8,128)} all-to-all(f32[32,64,256]{2,1,0:T(8,128)S(1)} %fusion.23), channel_id=1, replica_groups=mesh['group'=8,'dev'=32] {'dev'}, dimensions={0} | all-to-all | bytes 4194304 | tf_op jit(solution)/shard_map/cond/branch_0_fun/all_to_all | solution.py:410
  668.3 1.7 reduce_sum.59
  670.0 0.2 tile.4
  670.2 31.9 %all_to_all.92 = f32[32,64,256]{2,1,0:T(8,128)S(1)} all-to-all(f32[32,64,256]{2,1,0:T(8,128)S(1)} %tile.4), channel_id=1, replica_groups=mesh['group'=8,'dev'=32] {'dev'}, dimensions={0} | all-to-all | bytes 4194304 | tf_op jit(solution)/shard_map/cond/branch_0_fun/all_to_all | solution.py:412
  702.1 3.5 convolution_bitcast_fusion.k_ref
  705.6 7.9 %branch_0_fun.11 = f32[256,256]{1,0:T(8,128)S(1)} custom-call(f32[256,256]{1,0:T(8,128)S(1)} %convolution_bitcast_fusion.k_ref), custom_call_target="tpu_custom_call" | custom-call | tf_op jit(solution)/shard_map/cond/branch_0_fun/pallas_call | solution.py:76
  713.5 1.9 fusion.24
  715.4 3.9 multiply_reduce_fusion
  719.3 10.8 %all_to_all.93 = f32[32,1,256]{2,1,0:T(1,128)S(1)} all-to-all(f32[32,1,256]{2,1,0:T(1,128)S(1)} %broadcast_in_dim.0), channel_id=1, replica_groups=mesh['group'=8,'dev'=32] {'dev'}, dimensions={0} | all-to-all | bytes 65536 | tf_op jit(solution)/shard_map/cond/branch_0_fun/all_to_all | solution.py:410
  730.2 10.7 %all_to_all.94 = f32[32,1,256]{2,1,0:T(1,128)S(1)} all-to-all(f32[32,1,256]{2,1,0:T(1,128)S(1)} %tile.5), channel_id=1, replica_groups=mesh['group'=8,'dev'=32] {'dev'}, dimensions={0} | all-to-all | bytes 65536 | tf_op jit(solution)/shard_map/cond/branch_0_fun/all_to_all | solution.py:412
  741.0 2.0 fusion.2
  742.9 4.0 all-to-all-start.12
  746.9 0.8 copy.24
  747.8 16.5 %all-to-all-done.12 = f32[32,32,256]{2,1,0:T(8,128)S(1)} async-done(((f32[32,32,256]{2,1,0:T(8,128)}), f32[32,32,256]{2,1,0:T(8,128)S(1)}, u32[]{:S(2)}, u32[]{:S(2)}) %all-to-all-start.12) | async-done | bytes 1048608 | tf_op jit(solution)/shard_map/cond/branch_0_fun/all_to_all | solution.py:410
  764.5 0.6 copy.33
  765.1 1.9 copy.34
  (14 shorter events, 0.3 us)
Async XLA Ops:
  0.6 2.3 copy-start
  2.9 2.7 copy-start.2
  742.9 21.3 %all-to-all-start.12 = ((f32[32,32,256]{2,1,0:T(8,128)}), f32[32,32,256]{2,1,0:T(8,128)S(1)}, u32[]{:S(2)}, u32[]{:S(2)}) async-start(f32[32,32,256]{2,1,0:T(8,128)} %fusion.2), calls=%async_computation.12 | async-start | bytes 2097152 | tf_op jit(solution)/shard_map/cond/branch_0_fun/all_to_all | solution.py:410
  764.5 2.5 copy-start.1

commit v3 on v2

--- a/solution.py
+++ b/solution.py
@@ -105,7 +105,8 @@
         self.sent.append(c)
 
     def each(self, f):
-        for k in range(1, self.n):
+        h = self.n // 2
+        for k in sorted(range(1, self.n), key=lambda k: abs(k - h)):
             f(k, lax.rem(self.me + k, self.n))
 
     def scatter(self, src, buf, ss, rs):
@@ -128,16 +129,15 @@
         self.each(lambda k, q: rcopy(out.at[ds8(q, r)], out.at[ds8(q, r)], ss.at[k], rs.at[k], self.dev(self.me)).wait_recv())
 
 
-def ag_dev(g, me, x_ref, out, ss, rs, ls):
+def ag_tokens(g, me, x_ref, out, ss, rs, ls, sent):
     core = lax.rem(me, 2); x = lax.rem(me // 2, 4); y = me // 8
-    hr = x_ref.shape[0] // 2
     def did(yy, xx): return (g, (yy * 4 + xx) * 2 + core)
     def slot(yy, xx): return core * 16 + yy * 4 + xx
     xs = [lax.rem(x + k, 4) for k in (1, 2, 3)]; ys = [lax.rem(y + k, 4) for k in (1, 2, 3)]
     sib = (g, (y * 4 + x) * 2 + 1 - core)
     mine = slot(y, x)
     lc = pltpu.make_async_copy(x_ref, out.at[mine], ls); lc.start()
-    H = [pl.ds(0, hr), pl.ds(hr, hr)]
+    H = [pl.ds(0, 104), pl.ds(104, 96)]
     sends = []
     def send(src, owner, h, dev):
         c = rcopy(src, out.at[owner, H[h]], ss.at[len(sends)], rs.at[owner, h], dev); c.start(); sends.append(c)
@@ -169,11 +169,45 @@
             for h in range(2):
                 wait(o, h); send(out.at[o, H[h]], o, h, sib)
     lc.wait()
-    def rest(j, c):
-        for h in range(2): wait((1 - core) * 16 + j, h)
-        return c
-    lax.fori_loop(0, 16, rest, 0)
-    for c in sends: c.wait_send()
+    sent.extend(sends)
+    def other_core():
+        def rest(j, c):
+            for h in range(2): wait((1 - core) * 16 + j, h)
+            return c
+        lax.fori_loop(0, 16, rest, 0)
+    return other_core
+
+
+def ag_block(g, me, x_ref, out, ss, rs, ls, sent, beside=lambda i: None):
+    core = lax.rem(me, 2); x = lax.rem(me // 2, 4); y = me // 8
+    hr = x_ref.shape[0] // 2
+    def did(yy, xx): return (g, (yy * 4 + xx) * 2 + core)
+    sib = (g, (y * 4 + x) * 2 + 1 - core)
+    lc = pltpu.make_async_copy(x_ref, out.at[core, y, x], ls); lc.start()
+    A, B = pl.ds(0, hr), pl.ds(hr, hr)
+    def send(src, dst, i, j, dev):
+        c = rcopy(src, dst, ss.at[i], rs.at[j], dev); c.start(); sent.append(c)
+    def wait(ref, j):
+        rcopy(ref, ref, ss.at[0], rs.at[j], sib).wait_recv()
+    for k in (1, 3, 2):
+        send(x_ref.at[A], out.at[core, y, x, A], k, 4 - k, did(y, lax.rem(x + k, 4)))
+        send(x_ref.at[B], out.at[core, y, x, B], 4 + k, 8 - k, did(lax.rem(y + k, 4), x))
+    beside(0)
+    lc.wait()
+    for k in (1, 2, 3): wait(out.at[core, y, lax.rem(x + k, 4), A], k)
+    row = out.at[core, y, :, A]
+    for k in (1, 3, 2): send(row, row, 8 + k, 12 - k, did(lax.rem(y + k, 4), x))
+    for k in (1, 2, 3): wait(out.at[core, lax.rem(y + k, 4), x, B], 4 + k)
+    column = out.at[core, :, x, B]
+    for k in (1, 3, 2): send(column, column, 12 + k, 16 - k, did(y, lax.rem(x + k, 4)))
+    beside(1)
+    for k in (1, 2, 3): wait(out.at[core, lax.rem(y + k, 4), :, A], 8 + k)
+    send(out.at[core, :, :, A], out.at[core, :, :, A], 0, 0, sib)
+    for k in (1, 2, 3): wait(out.at[core, :, lax.rem(x + k, 4), B], 12 + k)
+    send(out.at[core, :, :, B], out.at[core, :, :, B], 4, 4, sib)
+    beside(2)
+    wait(out.at[1 - core, :, :, A], 0)
+    wait(out.at[1 - core, :, :, B], 4)
 
 
 def token_blocks(hs_parts, gt_cat, own3, idx, tokall, b0):
@@ -199,8 +233,9 @@
     return G4, O4, Hs
 
 
-def merge_kernel(hs_in, gt_in, idx_in, coef, basis, state, tok, tokall, M, Gown, ysrc, Y, A, S, X, Z, W0, W0S, UP, SB, HB, UB, U, VP, VB, V, KP, KB, K,
-                 CF, CSB, CHB, CB, SQ, SQB, ag_s, ag_r, ag_l, bs, us, ur, us2, ur2, vs, vr, vs2, vr2, ks, kr, ks2, kr2, cs, cr, qs, qr, zs, zr):
+def merge_kernel(hs_in, gt_in, idx_in, coef, basis, state, tok, tokall, M, Gown, ysrc, Y, A, S, X, Z, W0, W0S, UP0, SB0, HB0, UB0, U0,
+                 UP, SB, HB, UB, U, VP, VB, V, KP, KB, K, CF, CSB, CHB, CB, SQ, SQB,
+                 ag_s, ag_r, ag_l, ys, yr, bs, br, us, ur, us2, ur2, vs, vr, vs2, vr2, ks, kr, ks2, kr2, cs, cr, qs, qr, zs, zr):
     g = lax.axis_index("group"); d = lax.axis_index("dev")
     core = lax.rem(d, 2); p = d // 2
     sib = (g, 2 * p + 1 - core)
@@ -225,7 +260,7 @@
     tok[192:200, :] = jnp.broadcast_to(idx + 32 * lax.rem(p, 4), (8, 128)).astype(F32)
     half = lambda c, n: pl.ds(pl.multiple_of(c * n, 8), n)
     pl.semaphore_wait(b, 23)
-    ag_dev(g, d, tok, tokall, ag_s.at[0], ag_r.at[0], ag_l.at[0])
+    other_core = ag_tokens(g, d, tok, tokall, ag_s, ag_r, ag_l.at[3], sent)
     hs_parts = split3(tok[0:128, :])
     h, m, l = split3(tok[128:192, :].T)
     gt_cat = jnp.concatenate([h, h, m, h, m, l], axis=1)
@@ -249,21 +284,27 @@
             M[ds8(4 * q + s, 32), 0:128] = mr[0:32]
             M[ds8(4 * q + s, 32), 128:256] = mr[32:64]
         return c
-    lax.fori_loop(0, 8, four, 0)
+    four(4 * core, 0)
+    other_core()
+    four(4 - 4 * core, 0)
+    def later(i):
+        def two(j, c):
+            return four(4 * j + i + 1, c)
+        lax.fori_loop(0, 2, two, 0)
     y0, y1 = Gown[0], Gown[4]
     ysrc[0] = jnp.concatenate([(y1 if s % 2 else y0)[:, 32 * (s // 2):32 * (s // 2) + 32] for s in range(8)], axis=1)
     for it in range(3):
-        ag_dev(g, d, ysrc.at[it], Y.at[it], ag_s.at[it + 1], ag_r.at[it + 1], ag_l.at[it + 1])
+        ag_block(g, d, ysrc.at[it], Y.at[it], ys.at[it], yr.at[it], ag_l.at[it], sent, later if it == 0 else lambda i: None)
         if it < 2:
             acc = jnp.zeros((32, 256), F32)
             for q in range(8):
-                acc = acc + mm(Gown[q], Y[it, 4 * q:4 * q + 4, :, :].reshape(128, 256))
+                acc = acc + mm(Gown[q], Y[it, q // 4, q % 4].reshape(128, 256))
             ysrc[it + 1] = acc
     def zpart(q, acc):
-        yb = Y[2, pl.ds(8 * q, 8), :, :].reshape(256, 256)
+        yb = Y[2, q // 2, pl.ds(2 * lax.rem(q, 2), 2)].reshape(256, 256)
         return acc + mm(yb, M[ds8(q, 256), :], 0, 0)
     def gram(q, acc):
-        yb = Y[2, pl.ds(8 * q, 8), :, :].reshape(256, 256)
+        yb = Y[2, q // 2, pl.ds(2 * lax.rem(q, 2), 2)].reshape(256, 256)
         return acc + mm(yb, yb, 0, 0)
     zero = jnp.zeros((256, 256), F32)
     z1 = lax.fori_loop(0, 4, zpart, zero)
@@ -294,81 +335,121 @@
     S[...] = mm(W, z1)
     AG.collect(X, 32, zs.at[pl.ds(8, 8)], zr.at[pl.ds(8, 8)])
     xt = X[...].T
-    for it in range(3):
-        UP[it] = mm(S[...], xt)
-        to_sib = rcopy(UP.at[it, half(1 - core, 128)], SB.at[it], bs.at[2 * it], bs.at[8 + 2 * it], sib)
-        to_sib.start()
-        sent.append(to_sib)
+    def to_sibling(src, dst, i):
+        c = rcopy(src, dst, bs.at[i], br.at[i], sib)
+        c.start()
+        sent.append(c)
+        return c
+    UP0[...] = mm(S[...], xt)
+    first = to_sibling(UP0.at[half(1 - core, 128)], SB0, 0)
+    @pl.when(g > 0)
+    def _():
+        rcopy(W0.at[ds8(g, 32)], W0.at[ds8(g, 32)], zs.at[0], zr.at[16], (g, d)).wait_recv()
+    AG.spread(W0.at[ds8(g, 32)], W0, 32, zs.at[pl.ds(24, 8)], zr.at[pl.ds(24, 8)])
+    first.wait_recv()
+    HB0[...] = UP0[half(core, 128), :] + SB0[...]
+    AC.scatter(HB0, UB0, us.at[4], ur.at[4])
+    uh = U0.at[half(core, 128)]
+    uh[ds8(p, 8), :] = AC.gather_sum(HB0, UB0, us.at[4], ur.at[4])
+    AC.spread(uh.at[ds8(p, 8)], uh, 8, us2.at[4], ur2.at[4])
+    AC.collect(uh, 8, us2.at[4], ur2.at[4])
+    first = to_sibling(uh, uh, 1)
+    AG.collect(W0, 32, zs.at[pl.ds(24, 8)], zr.at[pl.ds(24, 8)])
+    first.wait_recv()
+    u0 = mm(U0[...], W0[...], 1, 1)
+    flying = {}
+    def p1(it, h):
+        j = 2 * it - 2 + h
+        UP[j] = mm(S[...], V[2 * it - 2 + h])
+        flying[j] = to_sibling(UP.at[j, half(1 - core, 128)], SB.at[j], 2 + 2 * j)
+    def p2(it, h):
+        j = 2 * it - 2 + h
+        flying[j].wait_recv()
+        HB[j] = UP[j, half(core, 128), :] + SB[j]
+        AC.scatter(HB.at[j], UB.at[j], us.at[j], ur.at[j])
+    def p3(it, h):
+        j = 2 * it - 2 + h
+        uh = U.at[j, half(core, 128)]
+        uh[ds8(p, 8), :] = AC.gather_sum(HB.at[j], UB.at[j], us.at[j], ur.at[j])
+        AC.spread(uh.at[ds8(p, 8)], uh, 8, us2.at[j], ur2.at[j])
+    def p4(it, h):
+        j = 2 * it - 2 + h
+        uh = U.at[j, half(core, 128)]
+        AC.collect(uh, 8, us2.at[j], ur2.at[j])
+        flying[j] = to_sibling(uh, uh, 3 + 2 * j)
+    def p5(it, h):
+        v = 2 * it + h
         if it == 0:
-            @pl.when(g > 0)
-            def _():
-                rcopy(W0.at[ds8(g, 32)], W0.at[ds8(g, 32)], zs.at[0], zr.at[16], (g, d)).wait_recv()
-            AG.spread(W0.at[ds8(g, 32)], W0, 32, zs.at[pl.ds(24, 8)], zr.at[pl.ds(24, 8)])
-        to_sib.wait_recv()
-        HB[it] = UP[it, half(core, 128), :] + SB[it]
-        AC.scatter(HB.at[it], UB.at[it], us.at[it], ur.at[it])
-        uh = U.at[it, half(core, 128)]
-        uh[ds8(p, 8), :] = AC.gather_sum(HB.at[it], UB.at[it], us.at[it], ur.at[it])
-        AC.spread(uh.at[ds8(p, 8)], uh, 8, us2.at[it], ur2.at[it])
-        AC.collect(uh, 8, us2.at[it], ur2.at[it])
-        swap = rcopy(uh, uh, bs.at[2 * it + 1], bs.at[9 + 2 * it], sib)
-        swap.start()
-        sent.append(swap)
-        swap.wait_recv()
-        u = U[it]
-        if it == 2:
-            mine = core * 16 + p
-            KP[...] = mm(u, u, 0, 0)
-            KB[ds8(g, 8), :] = KP[ds8(mine, 8), :]
-            AG.spread(KP.at[ds8(mine, 8)], KB, 8, ks, kr)
-        VP[it] = mm(S[...], u, 0, 0)
-        AG.scatter(VP.at[it], VB.at[it], vs.at[it], vr.at[it])
-        if it == 2:
-            AG.collect(KB, 8, ks, kr)
-            acc = KB[0:8, :]
-            for q in range(1, 8):
-                acc = acc + KB[8 * q:8 * q + 8, :]
-            kh = K.at[half(core, 128)]
-            kh[ds8(p, 8), :] = acc
-            AC.spread(kh.at[ds8(p, 8)], kh, 8, ks2, kr2)
-        V[it, ds8(g, 32), :] = AG.gather_sum(VP.at[it], VB.at[it], vs.at[it], vr.at[it])
-        AG.spread(V.at[it, ds8(g, 32)], V.at[it], 32, vs2.at[it], vr2.at[it])
-        if it == 2:
-            AC.collect(kh, 8, ks2, kr2)
-            swap_k = rcopy(kh, kh, bs.at[6], bs.at[14], sib)
-            swap_k.start()
-            sent.append(swap_k)
-            swap_k.wait_recv()
-            A[...] = K[...]
-            chol_inv_body(A, 0, 3)
-        AG.collect(V.at[it], 32, vs2.at[it], vr2.at[it])
-        if it == 0:
-            AG.collect(W0, 32, zs.at[pl.ds(24, 8)], zr.at[pl.ds(24, 8)])
-            xt = mm(V[0], W0[...], 1, 1)
+            u = u0[:, 128 * h:128 * h + 128]
         else:
-            xt = V[it]
-    def cpart(q, c):
-        CF[ds8(q, 256), :] = mm(M[ds8(q, 256), :], V[2])
-        return c
-    lax.fori_loop(0, 4, cpart, 0)
-    csib = rcopy(CF.at[half(1 - core, 512)], CSB, bs.at[7], bs.at[15], sib)
-    csib.start()
-    sent.append(csib)
+            if flying[v - 2] is not None:
+                flying[v - 2].wait_recv()
+            u = U[v - 2]
+        VP[v] = mm(S[...], u, 0, 0)
+        AG.scatter(VP.at[v], VB.at[v], vs.at[v], vr.at[v])
+    def p6(it, h):
+        v = 2 * it + h
+        V[v, ds8(g, 32), :] = AG.gather_sum(VP.at[v], VB.at[v], vs.at[v], vr.at[v])
+        AG.spread(V.at[v, ds8(g, 32)], V.at[v], 32, vs2.at[v], vr2.at[v])
+    def p7(it, h):
+        v = 2 * it + h
+        AG.collect(V.at[v], 32, vs2.at[v], vr2.at[v])
+    p5(0, 0); p5(0, 1); p6(0, 0); p6(0, 1); p7(0, 0)
+    p1(1, 0); p2(1, 0); p3(1, 0); p4(1, 0); p7(0, 1)
+    for n in range(3, 6):
+        a, c = (n // 2, n % 2), ((n - 1) // 2, (n - 1) % 2)
+        p1(*a); p5(*c); p2(*a); p3(*a); p6(*c); p4(*a)
+        if n < 5:
+            p7(*c)
+    def coordinates(h):
+        def cpart(q, c):
+            CF[h, ds8(q, 256), :] = mm(M[ds8(q, 256), :], V[4 + h])
+            return c
+        lax.fori_loop(0, 4, cpart, 0)
+        return to_sibling(CF.at[h, half(1 - core, 512)], CSB.at[h], 11 + h)
+    def coordinates_out(h, c):
+        c.wait_recv()
+        CHB[h] = CF[h, half(core, 512), :] + CSB[h]
+        AC.scatter(CHB.at[h], CB.at[h], cs.at[h], cr.at[h])
+    mine = core * 16 + p
+    flying[3].wait_recv()
+    flying[3] = None
+    u = jnp.concatenate([U[2], U[3]], axis=1)
+    KP[...] = mm(u, u, 0, 0)
+    KB[ds8(g, 8), :] = KP[ds8(mine, 8), :]
+    AG.spread(KP.at[ds8(mine, 8)], KB, 8, ks, kr)
+    p5(2, 1)
+    AG.collect(KB, 8, ks, kr)
+    acc = KB[0:8, :]
+    for q in range(1, 8):
+        acc = acc + KB[8 * q:8 * q + 8, :]
+    kh = K.at[half(core, 128)]
+    kh[ds8(p, 8), :] = acc
+    AC.spread(kh.at[ds8(p, 8)], kh, 8, ks2, kr2)
+    p7(2, 0)
+    c0 = coordinates(0)
+    p6(2, 1)
+    AC.collect(kh, 8, ks2, kr2)
+    swap_k = to_sibling(kh, kh, 10)
+    coordinates_out(0, c0)
+    swap_k.wait_recv()
+    A[...] = K[...]
+    chol_inv_body(A, 0, 3)
+    p7(2, 1)
+    c1 = coordinates(1)
     chol_inv_body(A, 3, 5)
-    csib.wait_recv()
-    CHB[...] = CF[half(core, 512), :] + CSB[...]
-    AC.scatter(CHB, CB, cs, cr)
+    coordinates_out(1, c1)
     chol_inv_body(A, 5, 8)
     diag = jnp.sum(jnp.where(col == row, A[...], 0.0), axis=0, keepdims=True)
     hi = jnp.max(diag, axis=1, keepdims=True); lo = jnp.min(diag, axis=1, keepdims=True)
     state[...] = jnp.broadcast_to(jnp.where(hi < SPAN * lo, 1.0, 0.0), (8, 128))
     W = jnp.where(tri, A[...], 0.0)
-    mt = mm(V[2], W, 1, 1)
+    mt = mm(jnp.concatenate([V[4], V[5]], axis=1), W, 1, 1)
     SQ[0] = jnp.broadcast_to(jnp.sum(mt * mt, axis=0, keepdims=True), (8, 256))
     qsib = rcopy(SQ.at[0], SQ.at[1], qs.at[0], qr.at[0], sib)
     qsib.start()
     sent.append(qsib)
-    cfs = mm(AC.gather_sum(CHB, CB, cs, cr), W, 1, 1)
+    cfs = mm(jnp.concatenate([AC.gather_sum(CHB.at[h], CB.at[h], cs.at[h], cr.at[h]) for h in range(2)], axis=1), W, 1, 1)
     qsib.wait_recv()
     SQB[ds8(p, 8), :] = SQ[0] + SQ[1]
     AC.spread(SQB.at[ds8(p, 8)], SQB, 8, qs, qr)
@@ -390,13 +471,16 @@
         out_shape=[jax.ShapeDtypeStruct((32, 256), F32), jax.ShapeDtypeStruct((256, 256), F32), jax.ShapeDtypeStruct((8, 128), F32)],
         in_specs=[VM, VM, VM], out_specs=[VM, VM, VM],
         scratch_shapes=[
-            V(200, 128), V(32, 200, 128), V(1024, 256), V(8, 32, 128), V(3, 32, 256), V(3, 32, 32, 256),
+            V(200, 128), V(32, 200, 128), V(1024, 256), V(8, 32, 128), V(3, 32, 256), V(3, 2, 4, 4, 32, 256),
             V(256, 256), V(256, 256), V(256, 256), V(256, 256), V(256, 256), V(256, 256),
-            V(3, 256, 256), V(3, 128, 256), V(3, 128, 256), V(3, 16, 8, 256), V(3, 256, 256), V(3, 256, 256), V(3, 8, 32, 256), V(3, 256, 256),
-            V(256, 256), V(64, 256), V(256, 256), V(1024, 256), V(512, 256), V(512, 256), V(16, 32, 256), V(2, 8, 256), V(128, 256),
-            D((4, 80)), D((4, 32, 2)), D((4,)), D((16,)),
-            D((3, 16)), D((3, 16)), D((3, 16)), D((3, 16)), D((3, 8)), D((3, 8)), D((3, 8)), D((3, 8)),
-            D((8,)), D((8,)), D((16,)), D((16,)), D((16,)), D((16,)), D((16,)), D((16,)), D((32,)), D((32,)),
+            V(256, 256), V(128, 256), V(128, 256), V(16, 8, 256), V(256, 256),
+            V(4, 256, 128), V(4, 128, 128), V(4, 128, 128), V(4, 16, 8, 128), V(4, 256, 128),
+            V(6, 256, 128), V(6, 8, 32, 128), V(6, 256, 128),
+            V(256, 256), V(64, 256), V(256, 256),
+            V(2, 1024, 128), V(2, 512, 128), V(2, 512, 128), V(2, 16, 32, 128), V(2, 8, 256), V(128, 256),
+            D((80,)), D((32, 2)), D((4,)), D((3, 16)), D((3, 16)), D((16,)), D((16,)),
+            D((5, 16)), D((5, 16)), D((5, 16)), D((5, 16)), D((6, 8)), D((6, 8)), D((6, 8)), D((6, 8)),
+            D((8,)), D((8,)), D((16,)), D((16,)), D((2, 16)), D((2, 16)), D((16,)), D((16,)), D((32,)), D((32,)),
         ],
         compiler_params=pltpu.CompilerParams(collective_id=1, has_side_effects=True, vmem_limit_bytes=56 << 20),
     )(hs, gt, idx)

time: 775 us -> 746 us (0.963)
  Pallas kernels: 251 us -> 234 us
  blocking collectives: 416 us -> 403 us
    pallas_call x1, Pallas kernels: 204 us -> 187 us  [merge_all(): pl.pallas_call(merge_kernel, out_shape=[jax.ShapeDtypeStruct((32, 256), F...]
    all_to_all x1, blocking collectives: 35 us -> 23 us  [merge_slow(): block = lax.all_to_all(rows, 'dev', split_axis=1, concat_axis=0, tiled=True)]
where the time goes in v3:
time: 746 us; the launch traced here: 737 us
  blocking collectives  403 us (54%)
  Pallas kernels  234 us (31%)
  matrix products  62.3 us (8%)
  waiting for transfers between devices  16.5 us (2%)
  other arithmetic  7.86 us (1%)
    all_to_all x6, blocking collectives, gather(): lax.all_to_all(jnp.tile(x, (n, 1)), axis, split_axis=0, concat_axis=0, ti...  217 us
    pallas_call x1, Pallas kernels, merge_all(): pl.pallas_call(merge_kernel, out_shape=[jax.ShapeDtypeStruct((32, 256), F...  187 us
    all_to_all x5, blocking collectives, sum_parts(): lax.all_to_all(x, axis, split_axis=0, concat_axis=0, tiled=True)  164 us
    dot_general x24, matrix products, mm(): lax.dot_general(a, b, (((ca,), (cb,)), ((), ())), precision=HI, preferred...  57.6 us
    pallas_call x6, Pallas kernels, chol_inv(): pl.pallas_call(chol_kernel, out_shape=jax.ShapeDtypeStruct((256, 256), F3...  47.3 us
    all_to_all x1, blocking collectives, merge_slow(): block = lax.all_to_all(rows, 'dev', split_axis=1, concat_axis=0, tiled=True)  23 us
    all_to_all x1, waiting for transfers between devices, sum_parts(): lax.all_to_all(x, axis, split_axis=0, concat_axis=0, tiled=True)  16.5 us
  transfers between devices with their start and end apart: 1, of which 1 were waited for; matrix products, arithmetic and copies ran while one was open for 0% of the time, Pallas kernels for 0%

profile of v3, /device:TPU:1, one launch (start us, length us, event | category | flops | bytes accessed | tf_op | source)
XLA Modules:
  0.0 737.5 jit_solution(1746996713133980949)
XLA Ops:
  0.6 2.0 fusion.26.gt_in
  2.7 0.2 copy-done
  2.9 2.7 fusion.25.hs_in
  5.6 187.1 %shard_map.70 = (f32[32,256]{1,0:T(8,128)S(1)}, f32[256,256]{1,0:T(8,128)}, f32[8,128]{1,0:T(8,128)}) custom-call(f32[128,128]{1,0:T(8,128)S(1)} %fusion.25.hs_in, f32[64,128]{1,0:T(8,128)S(1)} %fusion.26.gt_in, s32[1,128]{1,0:T(1,128)S(1)} %copy-done.2), custom_call_target="tpu_custom_call" | custom-call | tf_op jit(solution)/shard_map/pallas_call | solution.py:469
  192.7 1.2 slice.16
  194.6 540.2 %conditional.1 = ((f32[32,256]{1,0:T(8,128)S(1)}, f32[256,256]{1,0:T(8,128)})) conditional(s32[]{:T(128)} %bitcast.20, (s32[1,128]{1,0:T(1,128)S(1)}, f32[64,128]{1,0:T(8,128)S(1)}, f32[128,128]{1,0:T(8,128)S(1)}) %tuple.33, (f32[32,256]{1,0:T(8,128)S(1)}, f32[256,256]{1,0:T(8,128)}) %tuple.15), branch_computations={%region_0.0_spmd, %region_8.0_spmd} | conditional | flops 35839672320 | bytes 167059008 | solution.py:522
  194.7 1.0 convolution_multiply_fusion
  195.7 0.3 mul.31
  196.0 0.6 copy.17
  196.6 23.0 %all_to_all.83 = f32[32,32,256]{2,0,1:T(8,128)S(1)} all-to-all(f32[32,32,256]{2,0,1:T(8,128)S(1)} %copy.17), channel_id=1, replica_groups=mesh['group'=8,'dev'=32] {'dev'}, dimensions={1} | all-to-all | bytes 2097152 | tf_op jit(solution)/shard_map/cond/branch_0_fun/all_to_all | solution.py:502
  219.6 3.8 fusion
  223.4 54.7 %all_to_all.84 = f32[32,32,1024]{2,1,0:T(8,128)} all-to-all(f32[32,32,1024]{2,1,0:T(8,128)S(1)} %fusion), channel_id=1, replica_groups=mesh['group'=8,'dev'=32] {'dev'}, dimensions={0} | all-to-all | bytes 8388608 | tf_op jit(solution)/shard_map/cond/branch_0_fun/all_to_all | solution.py:494
  278.2 2.4 reduce_sum.56
  280.6 0.5 tile.0
  281.1 55.2 %all_to_all.85 = f32[32,32,1024]{2,1,0:T(8,128)S(1)} all-to-all(f32[32,32,1024]{2,1,0:T(8,128)S(1)} %tile.0), channel_id=1, replica_groups=mesh['group'=8,'dev'=32] {'dev'}, dimensions={0} | all-to-all | bytes 8388608 | tf_op jit(solution)/shard_map/cond/branch_0_fun/all_to_all | solution.py:496
  336.3 1.8 fusion.6.k_ref
  338.2 7.9 %branch_0_fun.6 = f32[256,256]{1,0:T(8,128)S(1)} custom-call(f32[256,256]{1,0:T(8,128)S(1)} %fusion.6.k_ref), custom_call_target="tpu_custom_call" | custom-call | tf_op jit(solution)/shard_map/cond/branch_0_fun/pallas_call | solution.py:76
  346.0 1.0 fusion.4
  347.1 3.4 fusion.13
  350.5 2.2 fusion.14.k_ref
  352.8 7.9 %branch_0_fun.7 = f32[256,256]{1,0:T(8,128)S(1)} custom-call(f32[256,256]{1,0:T(8,128)S(1)} %fusion.14.k_ref), custom_call_target="tpu_custom_call" | custom-call | tf_op jit(solution)/shard_map/cond/branch_0_fun/pallas_call | solution.py:76
  360.6 1.0 fusion.15
  361.7 3.4 fusion.16
  365.1 1.8 fusion.17.k_ref
  366.9 8.0 %branch_0_fun.8 = f32[256,256]{1,0:T(8,128)S(1)} custom-call(f32[256,256]{1,0:T(8,128)S(1)} %fusion.17.k_ref), custom_call_target="tpu_custom_call" | custom-call | tf_op jit(solution)/shard_map/cond/branch_0_fun/pallas_call | solution.py:76
  375.0 1.0 fusion.18
  376.0 1.8 fusion.19
  377.8 0.2 tile.1
  378.0 54.9 %all_to_all.86 = f32[8,256,256]{2,1,0:T(8,128)S(1)} all-to-all(f32[8,256,256]{2,1,0:T(8,128)S(1)} %tile.1), channel_id=1, replica_groups=mesh['group'=8,'dev'=32] {'group'}, dimensions={0} | all-to-all | bytes 4194304 | tf_op jit(solution)/shard_map/cond/branch_0_fun/all_to_all | solution.py:496
  432.9 1.9 fusion.8
  434.8 33.8 %all_to_all.87 = f32[32,64,256]{2,1,0:T(8,128)} all-to-all(f32[32,64,256]{2,1,0:T(8,128)S(1)} %fusion.8), channel_id=1, replica_groups=mesh['group'=8,'dev'=32] {'dev'}, dimensions={0} | all-to-all | bytes 4194304 | tf_op jit(solution)/shard_map/cond/branch_0_fun/all_to_all | solution.py:494
  468.6 1.7 reduce_sum.57
  470.3 0.2 tile.2
  470.6 31.9 %all_to_all.88 = f32[32,64,256]{2,1,0:T(8,128)S(1)} all-to-all(f32[32,64,256]{2,1,0:T(8,128)S(1)} %tile.2), channel_id=1, replica_groups=mesh['group'=8,'dev'=32] {'dev'}, dimensions={0} | all-to-all | bytes 4194304 | tf_op jit(solution)/shard_map/cond/branch_0_fun/all_to_all | solution.py:496
  502.5 3.5 convolution_bitcast_fusion.4.k_ref
  506.0 7.9 %branch_0_fun.9 = f32[256,256]{1,0:T(8,128)S(1)} custom-call(f32[256,256]{1,0:T(8,128)S(1)} %convolution_bitcast_fusion.4.k_ref), custom_call_target="tpu_custom_call" | custom-call | tf_op jit(solution)/shard_map/cond/branch_0_fun/pallas_call | solution.py:76
  513.8 1.9 fusion.20
  515.8 3.7 convolution_bitcast_fusion.3
  519.4 1.9 fusion.21
  521.3 32.3 %all_to_all.89 = f32[32,64,256]{2,1,0:T(8,128)} all-to-all(f32[32,64,256]{2,1,0:T(8,128)S(1)} %fusion.21), channel_id=1, replica_groups=mesh['group'=8,'dev'=32] {'dev'}, dimensions={0} | all-to-all | bytes 4194304 | tf_op jit(solution)/shard_map/cond/branch_0_fun/all_to_all | solution.py:494
  553.6 1.7 reduce_sum.58
  555.3 0.2 tile.3
  555.6 31.9 %all_to_all.90 = f32[32,64,256]{2,1,0:T(8,128)S(1)} all-to-all(f32[32,64,256]{2,1,0:T(8,128)S(1)} %tile.3), channel_id=1, replica_groups=mesh['group'=8,'dev'=32] {'dev'}, dimensions={0} | all-to-all | bytes 4194304 | tf_op jit(solution)/shard_map/cond/branch_0_fun/all_to_all | solution.py:496
  587.4 3.5 convolution_bitcast_fusion.2.k_ref
  590.9 7.9 %branch_0_fun.10 = f32[256,256]{1,0:T(8,128)S(1)} custom-call(f32[256,256]{1,0:T(8,128)S(1)} %convolution_bitcast_fusion.2.k_ref), custom_call_target="tpu_custom_call" | custom-call | tf_op jit(solution)/shard_map/cond/branch_0_fun/pallas_call | solution.py:76
  598.8 1.9 fusion.22
  600.7 3.7 convolution_bitcast_fusion.1
  604.4 1.9 fusion.23
  606.3 32.3 %all_to_all.91 = f32[32,64,256]{2,1,0:T(8,128)} all-to-all(f32[32,64,256]{2,1,0:T(8,128)S(1)} %fusion.23), channel_id=1, replica_groups=mesh['group'=8,'dev'=32] {'dev'}, dimensions={0} | all-to-all | bytes 4194304 | tf_op jit(solution)/shard_map/cond/branch_0_fun/all_to_all | solution.py:494
  638.6 1.7 reduce_sum.59
  640.3 0.2 tile.4
  640.5 31.9 %all_to_all.92 = f32[32,64,256]{2,1,0:T(8,128)S(1)} all-to-all(f32[32,64,256]{2,1,0:T(8,128)S(1)} %tile.4), channel_id=1, replica_groups=mesh['group'=8,'dev'=32] {'dev'}, dimensions={0} | all-to-all | bytes 4194304 | tf_op jit(solution)/shard_map/cond/branch_0_fun/all_to_all | solution.py:496
  672.4 3.5 convolution_bitcast_fusion.k_ref
  675.9 7.9 %branch_0_fun.11 = f32[256,256]{1,0:T(8,128)S(1)} custom-call(f32[256,256]{1,0:T(8,128)S(1)} %convolution_bitcast_fusion.k_ref), custom_call_target="tpu_custom_call" | custom-call | tf_op jit(solution)/shard_map/cond/branch_0_fun/pallas_call | solution.py:76
  683.8 1.9 fusion.24
  685.7 3.9 multiply_reduce_fusion
  689.6 10.8 %all_to_all.93 = f32[32,1,256]{2,1,0:T(1,128)S(1)} all-to-all(f32[32,1,256]{2,1,0:T(1,128)S(1)} %broadcast_in_dim.0), channel_id=1, replica_groups=mesh['group'=8,'dev'=32] {'dev'}, dimensions={0} | all-to-all | bytes 65536 | tf_op jit(solution)/shard_map/cond/branch_0_fun/all_to_all | solution.py:494
  700.5 10.7 %all_to_all.94 = f32[32,1,256]{2,1,0:T(1,128)S(1)} all-to-all(f32[32,1,256]{2,1,0:T(1,128)S(1)} %tile.5), channel_id=1, replica_groups=mesh['group'=8,'dev'=32] {'dev'}, dimensions={0} | all-to-all | bytes 65536 | tf_op jit(solution)/shard_map/cond/branch_0_fun/all_to_all | solution.py:496
  711.3 2.0 fusion.2
  713.2 4.0 all-to-all-start.12
  717.2 0.8 copy.24
  718.0 16.5 %all-to-all-done.12 = f32[32,32,256]{2,1,0:T(8,128)S(1)} async-done(((f32[32,32,256]{2,1,0:T(8,128)}), f32[32,32,256]{2,1,0:T(8,128)S(1)}, u32[]{:S(2)}, u32[]{:S(2)}) %all-to-all-start.12) | async-done | bytes 1048608 | tf_op jit(solution)/shard_map/cond/branch_0_fun/all_to_all | solution.py:494
  734.8 0.6 copy.33
  735.4 1.9 copy.34
  (14 shorter events, 0.3 us)
Async XLA Ops:
  0.6 2.3 copy-start
  2.9 2.7 copy-start.2
  713.2 21.3 %all-to-all-start.12 = ((f32[32,32,256]{2,1,0:T(8,128)}), f32[32,32,256]{2,1,0:T(8,128)S(1)}, u32[]{:S(2)}, u32[]{:S(2)}) async-start(f32[32,32,256]{2,1,0:T(8,128)} %fusion.2), calls=%async_computation.12 | async-start | bytes 2097152 | tf_op jit(solution)/shard_map/cond/branch_0_fun/all_to_all | solution.py:494
  734.8 2.5 copy-start.1

commit v4 on v3

--- a/solution.py
+++ b/solution.py
@@ -501,13 +501,9 @@
     rows = mm(weighted.reshape(-1, 128), hs).reshape(DOC_DEV, 8192) * (1.0 / math.sqrt(8192))
     block = lax.all_to_all(rows, "dev", split_axis=1, concat_axis=0, tiled=True)
     G = total(mm(block, block, 1, 1))
-    Q = orth(G[:, :RANK])
-    for _ in range(ITERS):
-        Q = orth(mm(G, Q))
+    Q = lax.fori_loop(0, ITERS + 1, lambda _, Q: orth(mm(G, Q)), jnp.eye(1024, RANK, dtype=F32))
     stacked = gather(mm(Q, block, 0, 0), "group", 8)
-    Q = orth(total(mm(stacked, stacked[:RANK], 1, 1)))
-    for _ in range(ITERS):
-        Q = orth(total(mm(stacked, mm(stacked, Q, 0, 0))))
+    Q = lax.fori_loop(0, ITERS + 1, lambda _, Q: orth(total(mm(stacked, mm(stacked, Q, 0, 0)))), jnp.eye(2048, RANK, dtype=F32))
     merged = mm(Q, stacked, 0, 0)
     squares = total(jnp.broadcast_to(jnp.sum(merged * merged, axis=1)[None, :], (32, RANK)))[0]
     basis = merged * (1.0 / jnp.sqrt(squares / 8192.0 + 1e-06))[:, None]

time: 746 us -> 837 us (1.12)
  blocking collectives: 403 us -> 209 us
  waiting for transfers between devices: 16.5 us -> 197 us
  matrix products: 62.3 us -> 117 us
  starting transfers between devices: 3.97 us -> 28 us
  local copies, waits for them, and re-layouts: 7.11 us -> 27.8 us
    all_to_all x6 -> x1, blocking collectives: 217 us -> 10.7 us  [gather(): lax.all_to_all(jnp.tile(x, (n, 1)), axis, split_axis=0, concat_axis=0, ti...]
    all_to_all x0 -> x5, waiting for transfers between devices: none -> 180 us  [gather(): lax.all_to_all(jnp.tile(x, (n, 1)), axis, split_axis=0, concat_axis=0, ti...]
    dot_general x24 -> x26, matrix products: 57.6 us -> 114 us  [mm(): lax.dot_general(a, b, (((ca,), (cb,)), ((), ())), precision=HI, preferred...]
    all_to_all x0 -> x5, starting transfers between devices: none -> 23.4 us  [gather(): lax.all_to_all(jnp.tile(x, (n, 1)), axis, split_axis=0, concat_axis=0, ti...]
    all_to_all x5, blocking collectives: 164 us -> 175 us  [sum_parts(): lax.all_to_all(x, axis, split_axis=0, concat_axis=0, tiled=True)]
    dot_general x0 -> x3, local copies, waits for them, and re-layouts: none -> 8.66 us  [mm(): lax.dot_general(a, b, (((ca,), (cb,)), ((), ())), precision=HI, preferred...]
  transfers between devices with their start and end apart: 1 -> 6, of which waited for: 1 -> 6; matrix products, arithmetic and copies ran while one was open for 0% -> 0% of each run, Pallas kernels for 0% -> 0%
where the time goes in v4:
time: 837 us; the launch traced here: 827 us
  Pallas kernels  234 us (28%)
  blocking collectives  209 us (25%)
  waiting for transfers between devices  197 us (24%)
  matrix products  117 us (14%)
  starting transfers between devices  28 us (3%)
  local copies, waits for them, and re-layouts  27.8 us (3%)
  other arithmetic  11.6 us (1%)
    pallas_call x1, Pallas kernels, merge_all(): pl.pallas_call(merge_kernel, out_shape=[jax.ShapeDtypeStruct((32, 256), F...  187 us
    all_to_all x5, waiting for transfers between devices, gather(): lax.all_to_all(jnp.tile(x, (n, 1)), axis, split_axis=0, concat_axis=0, ti...  180 us
    all_to_all x5, blocking collectives, sum_parts(): lax.all_to_all(x, axis, split_axis=0, concat_axis=0, tiled=True)  175 us
    dot_general x26, matrix products, mm(): lax.dot_general(a, b, (((ca,), (cb,)), ((), ())), precision=HI, preferred...  114 us
    pallas_call x6, Pallas kernels, chol_inv(): pl.pallas_call(chol_kernel, out_shape=jax.ShapeDtypeStruct((256, 256), F3...  47.1 us
    all_to_all x1, blocking collectives, merge_slow(): block = lax.all_to_all(rows, 'dev', split_axis=1, concat_axis=0, tiled=True)  23.5 us
    all_to_all x5, starting transfers between devices, gather(): lax.all_to_all(jnp.tile(x, (n, 1)), axis, split_axis=0, concat_axis=0, ti...  23.4 us
  transfers between devices with their start and end apart: 6, of which 6 were waited for; matrix products, arithmetic and copies ran while one was open for 0% of the time, Pallas kernels for 0%

profile of v4, /device:TPU:1, one launch (start us, length us, event | category | flops | bytes accessed | tf_op | source)
XLA Modules:
  0.0 827.3 jit_solution(10589903421570578002)
XLA Ops:
  0.7 1.8 copy-done
  2.4 2.7 fusion.16.hs_in
  5.7 187.0 %shard_map.70 = (f32[32,256]{1,0:T(8,128)S(1)}, f32[256,256]{1,0:T(8,128)}, f32[8,128]{1,0:T(8,128)}) custom-call(f32[128,128]{1,0:T(8,128)S(1)} %fusion.16.hs_in, f32[64,128]{1,0:T(8,128)S(1)} %fusion.17.gt_in, s32[1,128]{1,0:T(1,128)S(1)} %copy-done.4), custom_call_target="tpu_custom_call" | custom-call | tf_op jit(solution)/shard_map/pallas_call | solution.py:469
  194.5 630.3 %conditional.1 = ((f32[32,256]{1,0:T(8,128)S(1)}, f32[256,256]{1,0:T(8,128)})) conditional(s32[]{:T(128)} %bitcast.13, (s32[1,128]{1,0:T(1,128)S(1)}, f32[64,128]{1,0:T(8,128)S(1)}, f32[128,128]{1,0:T(8,128)S(1)}) %tuple.65, (f32[32,256]{1,0:T(8,128)S(1)}, f32[256,256]{1,0:T(8,128)}) %tuple.23), branch_computations={%region_0.0_spmd, %region_10.0_spmd} | conditional | flops 18123489280 | bytes 120921992 | solution.py:518
  194.6 2.0 convolution_multiply_fusion
  196.6 2.5 mul.31
  199.1 1.8 copy.24
  200.9 23.5 %all_to_all.65 = f32[32,32,256]{2,0,1:T(8,128)S(1)} all-to-all(f32[32,32,256]{2,0,1:T(8,128)S(1)} %copy.24), channel_id=1, replica_groups=mesh['group'=8,'dev'=32] {'dev'}, dimensions={1} | all-to-all | bytes 2097152 | tf_op jit(solution)/shard_map/cond/branch_0_fun/all_to_all | solution.py:502
  224.4 3.8 fusion.1
  228.2 54.8 %all_to_all.66 = f32[32,32,1024]{2,1,0:T(8,128)} all-to-all(f32[32,32,1024]{2,1,0:T(8,128)S(1)} %fusion.1), channel_id=1, replica_groups=mesh['group'=8,'dev'=32] {'dev'}, dimensions={0} | all-to-all | bytes 8388608 | tf_op jit(solution)/shard_map/cond/branch_0_fun/all_to_all | solution.py:494
  283.0 2.4 reduce_sum.41
  285.4 2.5 tile.1
  287.9 4.8 all-to-all-start.4
  293.8 49.3 %all-to-all-done.4 = f32[32,32,1024]{2,1,0:T(8,128)} async-done(((f32[32,32,1024]{2,1,0:T(8,128)}), f32[32,32,1024]{2,1,0:T(8,128)}, u32[]{:S(2)}, u32[]{:S(2)}) %all-to-all-start.4) | async-done | bytes 4194336 | tf_op jit(solution)/shard_map/cond/branch_0_fun/all_to_all | solution.py:496
  343.1 51.6 %while.18 = (s32[]{:T(128)}, f32[1024,256]{1,0:T(8,128)}, f32[1024,1024]{1,0:T(8,128)}, s32[]{:T(128)}) while((s32[]{:T(128)}, f32[1024,256]{1,0:T(8,128)}, f32[1024,1024]{1,0:T(8,128)}, s32[]{:T(128)}) %tuple.53), condition=%wide.region_3.0_spmd, body=%wide.region_2.0_spmd.sunk | while | flops 4831838208 | bytes 9961525 | solution.py:504
  343.1 5.5 fusion.68
  348.6 1.8 fusion.69.k_ref
  350.5 7.9 eval_jaxpr.2
  358.3 2.0 fusion.70
  360.3 5.5 fusion.68
  365.8 1.8 fusion.69.k_ref
  367.7 7.9 eval_jaxpr.2
  375.5 2.0 fusion.70
  377.5 5.5 fusion.68
  383.0 1.8 fusion.69.k_ref
  384.8 7.9 eval_jaxpr.2
  392.7 2.0 fusion.70
  394.7 3.4 fusion.15
  399.5 4.3 all-to-all-start.5
  405.3 47.0 %all-to-all-done.5 = f32[8,256,256]{2,1,0:T(8,128)} async-done(((f32[8,256,256]{2,1,0:T(8,128)}), f32[8,256,256]{2,1,0:T(8,128)}, u32[]{:S(2)}, u32[]{:S(2)}) %all-to-all-start.5) | async-done | bytes 2097184 | tf_op jit(solution)/shard_map/cond/branch_0_fun/all_to_all | solution.py:496
  452.3 316.7 %while.19 = (s32[]{:T(128)}, f32[2048,256]{1,0:T(8,128)}, f32[2048,256]{1,0:T(8,128)}, s32[]{:T(128)}, f32[]{:T(128)}) while((s32[]{:T(128)}, f32[2048,256]{1,0:T(8,128)}, f32[2048,256]{1,0:T(8,128)}, s32[]{:T(128)}, f32[]{:T(128)}) %tuple.56), condition=%wide.region_6.0_spmd, body=%wide.region_4.0_spmd.sunk | while | flops 6442958848 | bytes 34734176 | solution.py:506
  452.7 5.7 fusion.79
  458.4 6.5 convolution_bitcast_fusion.4
  464.9 2.9 copy.35
  467.8 37.5 %all_to_all.69 = f32[32,64,256]{2,1,0:T(8,128)} all-to-all(f32[32,64,256]{2,1,0:T(8,128)} %bitcast.85), channel_id=1, replica_groups=mesh['group'=8,'dev'=32] {'dev'}, dimensions={0} | all-to-all | bytes 4194304 | tf_op jit(solution)/shard_map/cond/branch_0_fun/while/body/eval_jaxpr/all_to_all | solution.py:494
  508.6 4.7 all-to-all-start.1
  513.4 28.0 %all-to-all-done.1 = f32[32,64,256]{2,1,0:T(8,128)} async-done(((f32[32,64,256]{2,1,0:T(8,128)}), f32[32,64,256]{2,1,0:T(8,128)}, u32[]{:S(2)}, u32[]{:S(2)}) %all-to-all-start.1) | async-done | bytes 2097184 | tf_op jit(solution)/shard_map/cond/branch_0_fun/while/body/eval_jaxpr/all_to_all | solution.py:496
  541.3 5.7 convolution_bitcast_fusion.5.k_ref
  547.0 7.9 eval_jaxpr.3
  554.9 4.7 fusion.80
  559.6 5.7 fusion.79
  565.3 6.5 convolution_bitcast_fusion.4
  571.8 2.9 copy.35
  574.7 35.3 %all_to_all.69 = f32[32,64,256]{2,1,0:T(8,128)} all-to-all(f32[32,64,256]{2,1,0:T(8,128)} %bitcast.85), channel_id=1, replica_groups=mesh['group'=8,'dev'=32] {'dev'}, dimensions={0} | all-to-all | bytes 4194304 | tf_op jit(solution)/shard_map/cond/branch_0_fun/while/body/eval_jaxpr/all_to_all | solution.py:494
  613.3 4.7 all-to-all-start.1
  618.0 28.0 %all-to-all-done.1 = f32[32,64,256]{2,1,0:T(8,128)} async-done(((f32[32,64,256]{2,1,0:T(8,128)}), f32[32,64,256]{2,1,0:T(8,128)}, u32[]{:S(2)}, u32[]{:S(2)}) %all-to-all-start.1) | async-done | bytes 2097184 | tf_op jit(solution)/shard_map/cond/branch_0_fun/while/body/eval_jaxpr/all_to_all | solution.py:496
  646.0 5.7 convolution_bitcast_fusion.5.k_ref
  651.7 7.9 eval_jaxpr.3
  659.5 4.7 fusion.80
  664.3 5.7 fusion.79
  670.0 6.5 convolution_bitcast_fusion.4
  676.5 2.9 copy.35
  679.3 35.3 %all_to_all.69 = f32[32,64,256]{2,1,0:T(8,128)} all-to-all(f32[32,64,256]{2,1,0:T(8,128)} %bitcast.85), channel_id=1, replica_groups=mesh['group'=8,'dev'=32] {'dev'}, dimensions={0} | all-to-all | bytes 4194304 | tf_op jit(solution)/shard_map/cond/branch_0_fun/while/body/eval_jaxpr/all_to_all | solution.py:494
  717.9 4.7 all-to-all-start.1
  722.7 28.0 %all-to-all-done.1 = f32[32,64,256]{2,1,0:T(8,128)} async-done(((f32[32,64,256]{2,1,0:T(8,128)}), f32[32,64,256]{2,1,0:T(8,128)}, u32[]{:S(2)}, u32[]{:S(2)}) %all-to-all-start.1) | async-done | bytes 2097184 | tf_op jit(solution)/shard_map/cond/branch_0_fun/while/body/eval_jaxpr/all_to_all | solution.py:496
  750.6 5.7 convolution_bitcast_fusion.5.k_ref
  756.3 7.9 eval_jaxpr.3
  764.2 4.7 fusion.80
  769.1 5.7 multiply_reduce_fusion
  774.8 12.4 %all_to_all.67 = f32[32,1,256]{2,1,0:T(1,128)S(1)} all-to-all(f32[32,1,256]{2,1,0:T(1,128)S(1)} %broadcast_in_dim.0), channel_id=1, replica_groups=mesh['group'=8,'dev'=32] {'dev'}, dimensions={0} | all-to-all | bytes 65536 | tf_op jit(solution)/shard_map/cond/branch_0_fun/all_to_all | solution.py:494
  787.3 10.7 %all_to_all.68 = f32[32,1,256]{2,1,0:T(1,128)S(1)} all-to-all(f32[32,1,256]{2,1,0:T(1,128)S(1)} %tile.4), channel_id=1, replica_groups=mesh['group'=8,'dev'=32] {'dev'}, dimensions={0} | all-to-all | bytes 65536 | tf_op jit(solution)/shard_map/cond/branch_0_fun/all_to_all | solution.py:496
  798.0 3.2 fusion.3
  801.2 4.6 all-to-all-start.8
  806.7 16.5 %all-to-all-done.8 = f32[32,32,256]{2,1,0:T(8,128)} async-done(((f32[32,32,256]{2,1,0:T(8,128)}), f32[32,32,256]{2,1,0:T(8,128)}, u32[]{:S(2)}, u32[]{:S(2)}) %all-to-all-start.8) | async-done | bytes 1048608 | tf_op jit(solution)/shard_map/cond/branch_0_fun/all_to_all | solution.py:494
  (32 shorter events, 20.1 us)
Async XLA Ops:
  0.6 1.8 copy-start
  0.6 4.5 copy-start.2
  0.7 4.5 copy-start.3
  2.4 3.2 copy-start.4
  224.4 3.8 copy-start.1
  287.9 55.2 %all-to-all-start.4 = ((f32[32,32,1024]{2,1,0:T(8,128)}), f32[32,32,1024]{2,1,0:T(8,128)}, u32[]{:S(2)}, u32[]{:S(2)}) async-start(f32[32,32,1024]{2,1,0:T(8,128)} %tile.1), calls=%async_computation.4 | async-start | bytes 8388608 | tf_op jit(solution)/shard_map/cond/branch_0_fun/all_to_all | solution.py:496
  399.5 52.8 %all-to-all-start.5 = ((f32[8,256,256]{2,1,0:T(8,128)}), f32[8,256,256]{2,1,0:T(8,128)}, u32[]{:S(2)}, u32[]{:S(2)}) async-start(f32[8,256,256]{2,1,0:T(8,128)} %tile.2), calls=%async_computation.5 | async-start | bytes 4194304 | tf_op jit(solution)/shard_map/cond/branch_0_fun/all_to_all | solution.py:496
  508.6 32.7 %all-to-all-start.1 = ((f32[32,64,256]{2,1,0:T(8,128)}), f32[32,64,256]{2,1,0:T(8,128)}, u32[]{:S(2)}, u32[]{:S(2)}) async-start(f32[32,64,256]{2,1,0:T(8,128)} %tile.9), calls=%async_computation.1 | async-start | bytes 4194304 | tf_op jit(solution)/shard_map/cond/branch_0_fun/while/body/eval_jaxpr/all_to_all | solution.py:496
  613.3 32.7 %all-to-all-start.1 = ((f32[32,64,256]{2,1,0:T(8,128)}), f32[32,64,256]{2,1,0:T(8,128)}, u32[]{:S(2)}, u32[]{:S(2)}) async-start(f32[32,64,256]{2,1,0:T(8,128)} %tile.9), calls=%async_computation.1 | async-start | bytes 4194304 | tf_op jit(solution)/shard_map/cond/branch_0_fun/while/body/eval_jaxpr/all_to_all | solution.py:496
  717.9 32.7 %all-to-all-start.1 = ((f32[32,64,256]{2,1,0:T(8,128)}), f32[32,64,256]{2,1,0:T(8,128)}, u32[]{:S(2)}, u32[]{:S(2)}) async-start(f32[32,64,256]{2,1,0:T(8,128)} %tile.9), calls=%async_computation.1 | async-start | bytes 4194304 | tf_op jit(solution)/shard_map/cond/branch_0_fun/while/body/eval_jaxpr/all_to_all | solution.py:496
  801.2 22.0 %all-to-all-start.8 = ((f32[32,32,256]{2,1,0:T(8,128)}), f32[32,32,256]{2,1,0:T(8,128)}, u32[]{:S(2)}, u32[]{:S(2)}) async-start(f32[32,32,256]{2,1,0:T(8,128)} %fusion.3), calls=%async_computation.8 | async-start | bytes 2097152 | tf_op jit(solution)/shard_map/cond/branch_0_fun/all_to_all | solution.py:494

commit v5 on v4

--- a/solution.py
+++ b/solution.py
@@ -442,7 +442,7 @@
     chol_inv_body(A, 5, 8)
     diag = jnp.sum(jnp.where(col == row, A[...], 0.0), axis=0, keepdims=True)
     hi = jnp.max(diag, axis=1, keepdims=True); lo = jnp.min(diag, axis=1, keepdims=True)
-    state[...] = jnp.broadcast_to(jnp.where(hi < SPAN * lo, 1.0, 0.0), (8, 128))
+    state[0, 0] = jnp.max(jnp.where(hi < SPAN * lo, 1.0, 0.0))
     W = jnp.where(tri, A[...], 0.0)
     mt = mm(jnp.concatenate([V[4], V[5]], axis=1), W, 1, 1)
     SQ[0] = jnp.broadcast_to(jnp.sum(mt * mt, axis=0, keepdims=True), (8, 256))
@@ -468,8 +468,8 @@
     V = lambda *s: pltpu.VMEM(s, F32)
     return pl.pallas_call(
         merge_kernel,
-        out_shape=[jax.ShapeDtypeStruct((32, 256), F32), jax.ShapeDtypeStruct((256, 256), F32), jax.ShapeDtypeStruct((8, 128), F32)],
-        in_specs=[VM, VM, VM], out_specs=[VM, VM, VM],
+        out_shape=[jax.ShapeDtypeStruct((32, 256), F32), jax.ShapeDtypeStruct((256, 256), F32), jax.ShapeDtypeStruct((1, 1), F32)],
+        in_specs=[VM, VM, VM], out_specs=[VM, VM, pl.BlockSpec(memory_space=pltpu.SMEM)],
         scratch_shapes=[
             V(200, 128), V(32, 200, 128), V(1024, 256), V(8, 32, 128), V(3, 32, 256), V(3, 2, 4, 4, 32, 256),
             V(256, 256), V(256, 256), V(256, 256), V(256, 256), V(256, 256), V(256, 256),

time: 837 us -> 836 us (level)
  no operation moved by 1% of the time
where the time goes in v5:
time: 836 us; the launch traced here: 826 us
  Pallas kernels  234 us (28%)
  blocking collectives  209 us (25%)
  waiting for transfers between devices  197 us (24%)
  matrix products  117 us (14%)
  starting transfers between devices  28.1 us (3%)
  local copies, waits for them, and re-layouts  26.6 us (3%)
  other arithmetic  11.6 us (1%)
    pallas_call x1, Pallas kernels, merge_all(): pl.pallas_call(merge_kernel, out_shape=[jax.ShapeDtypeStruct((32, 256), F...  187 us
    all_to_all x5, waiting for transfers between devices, gather(): lax.all_to_all(jnp.tile(x, (n, 1)), axis, split_axis=0, concat_axis=0, ti...  180 us
    all_to_all x5, blocking collectives, sum_parts(): lax.all_to_all(x, axis, split_axis=0, concat_axis=0, tiled=True)  176 us
    dot_general x26, matrix products, mm(): lax.dot_general(a, b, (((ca,), (cb,)), ((), ())), precision=HI, preferred...  114 us
    pallas_call x6, Pallas kernels, chol_inv(): pl.pallas_call(chol_kernel, out_shape=jax.ShapeDtypeStruct((256, 256), F3...  47.1 us
    all_to_all x5, starting transfers between devices, gather(): lax.all_to_all(jnp.tile(x, (n, 1)), axis, split_axis=0, concat_axis=0, ti...  23.4 us
    all_to_all x1, blocking collectives, merge_slow(): block = lax.all_to_all(rows, 'dev', split_axis=1, concat_axis=0, tiled=True)  22.9 us
  transfers between devices with their start and end apart: 6, of which 6 were waited for; matrix products, arithmetic and copies ran while one was open for 0% of the time, Pallas kernels for 0%

profile of v5, /device:TPU:1, one launch (start us, length us, event | category | flops | bytes accessed | tf_op | source)
XLA Modules:
  0.0 825.7 jit_solution(14855668358706191620)
XLA Ops:
  0.7 1.8 copy-done
  2.4 2.7 fusion.16.hs_in
  5.7 187.0 %shard_map.70 = (f32[32,256]{1,0:T(8,128)S(1)}, f32[256,256]{1,0:T(8,128)}, f32[1,1]{1,0:T(1,128)}) custom-call(f32[128,128]{1,0:T(8,128)S(1)} %fusion.16.hs_in, f32[64,128]{1,0:T(8,128)S(1)} %fusion.17.gt_in, s32[1,128]{1,0:T(1,128)S(1)} %copy-done.4), custom_call_target="tpu_custom_call" | custom-call | tf_op jit(solution)/shard_map/pallas_call | solution.py:469
  193.2 630.0 %conditional.1 = ((f32[32,256]{1,0:T(8,128)S(1)}, f32[256,256]{1,0:T(8,128)})) conditional(s32[]{:T(128)} %bitcast.13, (s32[1,128]{1,0:T(1,128)S(1)}, f32[64,128]{1,0:T(8,128)S(1)}, f32[128,128]{1,0:T(8,128)S(1)}) %tuple.65, (f32[32,256]{1,0:T(8,128)S(1)}, f32[256,256]{1,0:T(8,128)}) %tuple.23), branch_computations={%region_0.0_spmd, %region_10.0_spmd} | conditional | flops 18123489280 | bytes 120921992 | solution.py:518
  193.3 1.9 convolution_multiply_fusion
  195.3 2.5 mul.31
  197.8 1.8 copy.24
  199.6 22.9 %all_to_all.65 = f32[32,32,256]{2,0,1:T(8,128)S(1)} all-to-all(f32[32,32,256]{2,0,1:T(8,128)S(1)} %copy.24), channel_id=1, replica_groups=mesh['group'=8,'dev'=32] {'dev'}, dimensions={1} | all-to-all | bytes 2097152 | tf_op jit(solution)/shard_map/cond/branch_0_fun/all_to_all | solution.py:502
  222.6 3.8 fusion.1
  226.4 54.8 %all_to_all.66 = f32[32,32,1024]{2,1,0:T(8,128)} all-to-all(f32[32,32,1024]{2,1,0:T(8,128)S(1)} %fusion.1), channel_id=1, replica_groups=mesh['group'=8,'dev'=32] {'dev'}, dimensions={0} | all-to-all | bytes 8388608 | tf_op jit(solution)/shard_map/cond/branch_0_fun/all_to_all | solution.py:494
  281.1 2.4 reduce_sum.41
  283.6 2.5 tile.1
  286.1 4.8 all-to-all-start.4
  291.9 49.3 %all-to-all-done.4 = f32[32,32,1024]{2,1,0:T(8,128)} async-done(((f32[32,32,1024]{2,1,0:T(8,128)}), f32[32,32,1024]{2,1,0:T(8,128)}, u32[]{:S(2)}, u32[]{:S(2)}) %all-to-all-start.4) | async-done | bytes 4194336 | tf_op jit(solution)/shard_map/cond/branch_0_fun/all_to_all | solution.py:496
  341.3 51.6 %while.18 = (s32[]{:T(128)}, f32[1024,256]{1,0:T(8,128)}, f32[1024,1024]{1,0:T(8,128)}, s32[]{:T(128)}) while((s32[]{:T(128)}, f32[1024,256]{1,0:T(8,128)}, f32[1024,1024]{1,0:T(8,128)}, s32[]{:T(128)}) %tuple.53), condition=%wide.region_3.0_spmd, body=%wide.region_2.0_spmd.sunk | while | flops 4831838208 | bytes 9961525 | solution.py:504
  341.3 5.5 fusion.68
  346.8 1.8 fusion.69.k_ref
  348.6 7.9 eval_jaxpr.2
  356.5 2.0 fusion.70
  358.5 5.5 fusion.68
  364.0 1.8 fusion.69.k_ref
  365.8 7.9 eval_jaxpr.2
  373.7 2.0 fusion.70
  375.7 5.5 fusion.68
  381.2 1.8 fusion.69.k_ref
  383.0 7.9 eval_jaxpr.2
  390.9 2.0 fusion.70
  392.8 3.4 fusion.15
  397.7 4.4 all-to-all-start.5
  403.6 46.8 %all-to-all-done.5 = f32[8,256,256]{2,1,0:T(8,128)} async-done(((f32[8,256,256]{2,1,0:T(8,128)}), f32[8,256,256]{2,1,0:T(8,128)}, u32[]{:S(2)}, u32[]{:S(2)}) %all-to-all-start.5) | async-done | bytes 2097184 | tf_op jit(solution)/shard_map/cond/branch_0_fun/all_to_all | solution.py:496
  450.3 317.2 %while.19 = (s32[]{:T(128)}, f32[2048,256]{1,0:T(8,128)}, f32[2048,256]{1,0:T(8,128)}, s32[]{:T(128)}, f32[]{:T(128)}) while((s32[]{:T(128)}, f32[2048,256]{1,0:T(8,128)}, f32[2048,256]{1,0:T(8,128)}, s32[]{:T(128)}, f32[]{:T(128)}) %tuple.56), condition=%wide.region_6.0_spmd, body=%wide.region_4.0_spmd.sunk | while | flops 6442958848 | bytes 34734176 | solution.py:506
  450.7 5.7 fusion.79
  456.4 6.5 convolution_bitcast_fusion.4
  462.9 2.9 copy.35
  465.8 38.0 %all_to_all.69 = f32[32,64,256]{2,1,0:T(8,128)} all-to-all(f32[32,64,256]{2,1,0:T(8,128)} %bitcast.85), channel_id=1, replica_groups=mesh['group'=8,'dev'=32] {'dev'}, dimensions={0} | all-to-all | bytes 4194304 | tf_op jit(solution)/shard_map/cond/branch_0_fun/while/body/eval_jaxpr/all_to_all | solution.py:494
  507.1 4.7 all-to-all-start.1
  511.9 28.0 %all-to-all-done.1 = f32[32,64,256]{2,1,0:T(8,128)} async-done(((f32[32,64,256]{2,1,0:T(8,128)}), f32[32,64,256]{2,1,0:T(8,128)}, u32[]{:S(2)}, u32[]{:S(2)}) %all-to-all-start.1) | async-done | bytes 2097184 | tf_op jit(solution)/shard_map/cond/branch_0_fun/while/body/eval_jaxpr/all_to_all | solution.py:496
  539.8 5.7 convolution_bitcast_fusion.5.k_ref
  545.5 7.9 eval_jaxpr.3
  553.4 4.7 fusion.80
  558.1 5.7 fusion.79
  563.8 6.5 convolution_bitcast_fusion.4
  570.3 2.9 copy.35
  573.2 35.3 %all_to_all.69 = f32[32,64,256]{2,1,0:T(8,128)} all-to-all(f32[32,64,256]{2,1,0:T(8,128)} %bitcast.85), channel_id=1, replica_groups=mesh['group'=8,'dev'=32] {'dev'}, dimensions={0} | all-to-all | bytes 4194304 | tf_op jit(solution)/shard_map/cond/branch_0_fun/while/body/eval_jaxpr/all_to_all | solution.py:494
  611.8 4.7 all-to-all-start.1
  616.5 28.0 %all-to-all-done.1 = f32[32,64,256]{2,1,0:T(8,128)} async-done(((f32[32,64,256]{2,1,0:T(8,128)}), f32[32,64,256]{2,1,0:T(8,128)}, u32[]{:S(2)}, u32[]{:S(2)}) %all-to-all-start.1) | async-done | bytes 2097184 | tf_op jit(solution)/shard_map/cond/branch_0_fun/while/body/eval_jaxpr/all_to_all | solution.py:496
  644.5 5.7 convolution_bitcast_fusion.5.k_ref
  650.2 7.9 eval_jaxpr.3
  658.0 4.7 fusion.80
  662.8 5.7 fusion.79
  668.5 6.5 convolution_bitcast_fusion.4
  674.9 2.9 copy.35
  677.8 35.3 %all_to_all.69 = f32[32,64,256]{2,1,0:T(8,128)} all-to-all(f32[32,64,256]{2,1,0:T(8,128)} %bitcast.85), channel_id=1, replica_groups=mesh['group'=8,'dev'=32] {'dev'}, dimensions={0} | all-to-all | bytes 4194304 | tf_op jit(solution)/shard_map/cond/branch_0_fun/while/body/eval_jaxpr/all_to_all | solution.py:494
  716.4 4.7 all-to-all-start.1
  721.1 28.0 %all-to-all-done.1 = f32[32,64,256]{2,1,0:T(8,128)} async-done(((f32[32,64,256]{2,1,0:T(8,128)}), f32[32,64,256]{2,1,0:T(8,128)}, u32[]{:S(2)}, u32[]{:S(2)}) %all-to-all-start.1) | async-done | bytes 2097184 | tf_op jit(solution)/shard_map/cond/branch_0_fun/while/body/eval_jaxpr/all_to_all | solution.py:496
  749.1 5.7 convolution_bitcast_fusion.5.k_ref
  754.8 7.9 eval_jaxpr.3
  762.7 4.7 fusion.80
  767.6 5.7 multiply_reduce_fusion
  773.3 12.4 %all_to_all.67 = f32[32,1,256]{2,1,0:T(1,128)S(1)} all-to-all(f32[32,1,256]{2,1,0:T(1,128)S(1)} %broadcast_in_dim.0), channel_id=1, replica_groups=mesh['group'=8,'dev'=32] {'dev'}, dimensions={0} | all-to-all | bytes 65536 | tf_op jit(solution)/shard_map/cond/branch_0_fun/all_to_all | solution.py:494
  785.8 10.7 %all_to_all.68 = f32[32,1,256]{2,1,0:T(1,128)S(1)} all-to-all(f32[32,1,256]{2,1,0:T(1,128)S(1)} %tile.4), channel_id=1, replica_groups=mesh['group'=8,'dev'=32] {'dev'}, dimensions={0} | all-to-all | bytes 65536 | tf_op jit(solution)/shard_map/cond/branch_0_fun/all_to_all | solution.py:496
  796.5 3.2 fusion.3
  799.7 4.6 all-to-all-start.8
  805.2 16.5 %all-to-all-done.8 = f32[32,32,256]{2,1,0:T(8,128)} async-done(((f32[32,32,256]{2,1,0:T(8,128)}), f32[32,32,256]{2,1,0:T(8,128)}, u32[]{:S(2)}, u32[]{:S(2)}) %all-to-all-start.8) | async-done | bytes 1048608 | tf_op jit(solution)/shard_map/cond/branch_0_fun/all_to_all | solution.py:494
  (31 shorter events, 18.9 us)
Async XLA Ops:
  0.6 1.8 copy-start
  0.6 4.5 copy-start.2
  0.7 4.5 copy-start.3
  2.4 3.2 copy-start.4
  222.6 3.8 copy-start.1
  286.1 55.2 %all-to-all-start.4 = ((f32[32,32,1024]{2,1,0:T(8,128)}), f32[32,32,1024]{2,1,0:T(8,128)}, u32[]{:S(2)}, u32[]{:S(2)}) async-start(f32[32,32,1024]{2,1,0:T(8,128)} %tile.1), calls=%async_computation.4 | async-start | bytes 8388608 | tf_op jit(solution)/shard_map/cond/branch_0_fun/all_to_all | solution.py:496
  397.7 52.6 %all-to-all-start.5 = ((f32[8,256,256]{2,1,0:T(8,128)}), f32[8,256,256]{2,1,0:T(8,128)}, u32[]{:S(2)}, u32[]{:S(2)}) async-start(f32[8,256,256]{2,1,0:T(8,128)} %tile.2), calls=%async_computation.5 | async-start | bytes 4194304 | tf_op jit(solution)/shard_map/cond/branch_0_fun/all_to_all | solution.py:496
  507.1 32.7 %all-to-all-start.1 = ((f32[32,64,256]{2,1,0:T(8,128)}), f32[32,64,256]{2,1,0:T(8,128)}, u32[]{:S(2)}, u32[]{:S(2)}) async-start(f32[32,64,256]{2,1,0:T(8,128)} %tile.9), calls=%async_computation.1 | async-start | bytes 4194304 | tf_op jit(solution)/shard_map/cond/branch_0_fun/while/body/eval_jaxpr/all_to_all | solution.py:496
  611.8 32.7 %all-to-all-start.1 = ((f32[32,64,256]{2,1,0:T(8,128)}), f32[32,64,256]{2,1,0:T(8,128)}, u32[]{:S(2)}, u32[]{:S(2)}) async-start(f32[32,64,256]{2,1,0:T(8,128)} %tile.9), calls=%async_computation.1 | async-start | bytes 4194304 | tf_op jit(solution)/shard_map/cond/branch_0_fun/while/body/eval_jaxpr/all_to_all | solution.py:496
  716.4 32.7 %all-to-all-start.1 = ((f32[32,64,256]{2,1,0:T(8,128)}), f32[32,64,256]{2,1,0:T(8,128)}, u32[]{:S(2)}, u32[]{:S(2)}) async-start(f32[32,64,256]{2,1,0:T(8,128)} %tile.9), calls=%async_computation.1 | async-start | bytes 4194304 | tf_op jit(solution)/shard_map/cond/branch_0_fun/while/body/eval_jaxpr/all_to_all | solution.py:496
  799.7 22.0 %all-to-all-start.8 = ((f32[32,32,256]{2,1,0:T(8,128)}), f32[32,32,256]{2,1,0:T(8,128)}, u32[]{:S(2)}, u32[]{:S(2)}) async-start(f32[32,32,256]{2,1,0:T(8,128)} %fusion.3), calls=%async_computation.8 | async-start | bytes 2097152 | tf_op jit(solution)/shard_map/cond/branch_0_fun/all_to_all | solution.py:494

commit v6 on v5

--- a/solution.py
+++ b/solution.py
@@ -259,14 +259,14 @@
     idx = idx_in[0:1, :]
     tok[192:200, :] = jnp.broadcast_to(idx + 32 * lax.rem(p, 4), (8, 128)).astype(F32)
     half = lambda c, n: pl.ds(pl.multiple_of(c * n, 8), n)
-    pl.semaphore_wait(b, 23)
-    other_core = ag_tokens(g, d, tok, tokall, ag_s, ag_r, ag_l.at[3], sent)
     hs_parts = split3(tok[0:128, :])
     h, m, l = split3(tok[128:192, :].T)
     gt_cat = jnp.concatenate([h, h, m, h, m, l], axis=1)
     drow = lax.broadcasted_iota(jnp.int32, (32, 128), 0)
     own = (jnp.broadcast_to(idx, (32, 128)) == drow).astype(BF)
     own3 = jnp.concatenate([own, own, own], axis=1)
+    pl.semaphore_wait(b, 23)
+    other_core = ag_tokens(g, d, tok, tokall, ag_s, ag_r, ag_l.at[3], sent)
     par = lax.rem(d, 4)
     gbase = pl.multiple_of((d // 4) * 8, 8)
     r8 = lax.broadcasted_iota(jnp.int32, (8, 128), 0)
@@ -449,10 +449,10 @@
     qsib = rcopy(SQ.at[0], SQ.at[1], qs.at[0], qr.at[0], sib)
     qsib.start()
     sent.append(qsib)
-    cfs = mm(jnp.concatenate([AC.gather_sum(CHB.at[h], CB.at[h], cs.at[h], cr.at[h]) for h in range(2)], axis=1), W, 1, 1)
     qsib.wait_recv()
     SQB[ds8(p, 8), :] = SQ[0] + SQ[1]
     AC.spread(SQB.at[ds8(p, 8)], SQB, 8, qs, qr)
+    cfs = mm(jnp.concatenate([AC.gather_sum(CHB.at[h], CB.at[h], cs.at[h], cr.at[h]) for h in range(2)], axis=1), W, 1, 1)
     AC.collect(SQB, 8, qs, qr)
     sq = SQB[0:8, :]
     for q in range(1, 16):

time: 836 us -> 833 us (level)
  no operation moved by 1% of the time
where the time goes in v6:
time: 833 us; the launch traced here: 824 us
  Pallas kernels  233 us (28%)
  blocking collectives  209 us (25%)
  waiting for transfers between devices  197 us (24%)
  matrix products  117 us (14%)
  starting transfers between devices  28 us (3%)
  local copies, waits for them, and re-layouts  26.6 us (3%)
  other arithmetic  11.6 us (1%)
    pallas_call x1, Pallas kernels, merge_all(): pl.pallas_call(merge_kernel, out_shape=[jax.ShapeDtypeStruct((32, 256), F...  186 us
    all_to_all x5, waiting for transfers between devices, gather(): lax.all_to_all(jnp.tile(x, (n, 1)), axis, split_axis=0, concat_axis=0, ti...  180 us
    all_to_all x5, blocking collectives, sum_parts(): lax.all_to_all(x, axis, split_axis=0, concat_axis=0, tiled=True)  175 us
    dot_general x26, matrix products, mm(): lax.dot_general(a, b, (((ca,), (cb,)), ((), ())), precision=HI, preferred...  114 us
    pallas_call x6, Pallas kernels, chol_inv(): pl.pallas_call(chol_kernel, out_shape=jax.ShapeDtypeStruct((256, 256), F3...  47.1 us
    all_to_all x5, starting transfers between devices, gather(): lax.all_to_all(jnp.tile(x, (n, 1)), axis, split_axis=0, concat_axis=0, ti...  23.4 us
    all_to_all x1, blocking collectives, merge_slow(): block = lax.all_to_all(rows, 'dev', split_axis=1, concat_axis=0, tiled=True)  22.4 us
  transfers between devices with their start and end apart: 6, of which 6 were waited for; matrix products, arithmetic and copies ran while one was open for 0% of the time, Pallas kernels for 0%

profile of v6, /device:TPU:1, one launch (start us, length us, event | category | flops | bytes accessed | tf_op | source)
XLA Modules:
  0.0 823.6 jit_solution(6840184089334966083)
XLA Ops:
  0.7 1.8 copy-done
  2.4 2.7 fusion.16.hs_in
  5.7 185.7 %shard_map.70 = (f32[32,256]{1,0:T(8,128)S(1)}, f32[256,256]{1,0:T(8,128)}, f32[1,1]{1,0:T(1,128)}) custom-call(f32[128,128]{1,0:T(8,128)S(1)} %fusion.16.hs_in, f32[64,128]{1,0:T(8,128)S(1)} %fusion.17.gt_in, s32[1,128]{1,0:T(1,128)S(1)} %copy-done.4), custom_call_target="tpu_custom_call" | custom-call | tf_op jit(solution)/shard_map/pallas_call | solution.py:469
  191.9 629.2 %conditional.1 = ((f32[32,256]{1,0:T(8,128)S(1)}, f32[256,256]{1,0:T(8,128)})) conditional(s32[]{:T(128)} %bitcast.13, (s32[1,128]{1,0:T(1,128)S(1)}, f32[64,128]{1,0:T(8,128)S(1)}, f32[128,128]{1,0:T(8,128)S(1)}) %tuple.65, (f32[32,256]{1,0:T(8,128)S(1)}, f32[256,256]{1,0:T(8,128)}) %tuple.23), branch_computations={%region_0.0_spmd, %region_10.0_spmd} | conditional | flops 18123489280 | bytes 120921992 | solution.py:518
  192.0 2.0 convolution_multiply_fusion
  194.0 2.5 mul.31
  196.5 1.8 copy.24
  198.3 22.4 %all_to_all.65 = f32[32,32,256]{2,0,1:T(8,128)S(1)} all-to-all(f32[32,32,256]{2,0,1:T(8,128)S(1)} %copy.24), channel_id=1, replica_groups=mesh['group'=8,'dev'=32] {'dev'}, dimensions={1} | all-to-all | bytes 2097152 | tf_op jit(solution)/shard_map/cond/branch_0_fun/all_to_all | solution.py:502
  220.8 3.8 fusion.1
  224.6 54.8 %all_to_all.66 = f32[32,32,1024]{2,1,0:T(8,128)} all-to-all(f32[32,32,1024]{2,1,0:T(8,128)S(1)} %fusion.1), channel_id=1, replica_groups=mesh['group'=8,'dev'=32] {'dev'}, dimensions={0} | all-to-all | bytes 8388608 | tf_op jit(solution)/shard_map/cond/branch_0_fun/all_to_all | solution.py:494
  279.3 2.4 reduce_sum.41
  281.8 2.5 tile.1
  284.3 4.8 all-to-all-start.4
  290.2 49.3 %all-to-all-done.4 = f32[32,32,1024]{2,1,0:T(8,128)} async-done(((f32[32,32,1024]{2,1,0:T(8,128)}), f32[32,32,1024]{2,1,0:T(8,128)}, u32[]{:S(2)}, u32[]{:S(2)}) %all-to-all-start.4) | async-done | bytes 4194336 | tf_op jit(solution)/shard_map/cond/branch_0_fun/all_to_all | solution.py:496
  339.5 51.6 %while.18 = (s32[]{:T(128)}, f32[1024,256]{1,0:T(8,128)}, f32[1024,1024]{1,0:T(8,128)}, s32[]{:T(128)}) while((s32[]{:T(128)}, f32[1024,256]{1,0:T(8,128)}, f32[1024,1024]{1,0:T(8,128)}, s32[]{:T(128)}) %tuple.53), condition=%wide.region_3.0_spmd, body=%wide.region_2.0_spmd.sunk | while | flops 4831838208 | bytes 9961525 | solution.py:504
  339.5 5.5 fusion.68
  345.0 1.8 fusion.69.k_ref
  346.8 7.9 eval_jaxpr.2
  354.7 2.0 fusion.70
  356.7 5.5 fusion.68
  362.2 1.8 fusion.69.k_ref
  364.0 7.9 eval_jaxpr.2
  371.9 2.0 fusion.70
  373.9 5.5 fusion.68
  379.4 1.8 fusion.69.k_ref
  381.2 7.9 eval_jaxpr.2
  389.1 2.0 fusion.70
  391.1 3.4 fusion.15
  395.9 4.3 all-to-all-start.5
  401.7 46.8 %all-to-all-done.5 = f32[8,256,256]{2,1,0:T(8,128)} async-done(((f32[8,256,256]{2,1,0:T(8,128)}), f32[8,256,256]{2,1,0:T(8,128)}, u32[]{:S(2)}, u32[]{:S(2)}) %all-to-all-start.5) | async-done | bytes 2097184 | tf_op jit(solution)/shard_map/cond/branch_0_fun/all_to_all | solution.py:496
  448.5 316.9 %while.19 = (s32[]{:T(128)}, f32[2048,256]{1,0:T(8,128)}, f32[2048,256]{1,0:T(8,128)}, s32[]{:T(128)}, f32[]{:T(128)}) while((s32[]{:T(128)}, f32[2048,256]{1,0:T(8,128)}, f32[2048,256]{1,0:T(8,128)}, s32[]{:T(128)}, f32[]{:T(128)}) %tuple.56), condition=%wide.region_6.0_spmd, body=%wide.region_4.0_spmd.sunk | while | flops 6442958848 | bytes 34734176 | solution.py:506
  448.9 5.7 fusion.79
  454.6 6.5 convolution_bitcast_fusion.4
  461.1 2.9 copy.35
  464.0 37.7 %all_to_all.69 = f32[32,64,256]{2,1,0:T(8,128)} all-to-all(f32[32,64,256]{2,1,0:T(8,128)} %bitcast.85), channel_id=1, replica_groups=mesh['group'=8,'dev'=32] {'dev'}, dimensions={0} | all-to-all | bytes 4194304 | tf_op jit(solution)/shard_map/cond/branch_0_fun/while/body/eval_jaxpr/all_to_all | solution.py:494
  505.0 4.7 all-to-all-start.1
  509.7 28.0 %all-to-all-done.1 = f32[32,64,256]{2,1,0:T(8,128)} async-done(((f32[32,64,256]{2,1,0:T(8,128)}), f32[32,64,256]{2,1,0:T(8,128)}, u32[]{:S(2)}, u32[]{:S(2)}) %all-to-all-start.1) | async-done | bytes 2097184 | tf_op jit(solution)/shard_map/cond/branch_0_fun/while/body/eval_jaxpr/all_to_all | solution.py:496
  537.7 5.7 convolution_bitcast_fusion.5.k_ref
  543.4 7.9 eval_jaxpr.3
  551.3 4.7 fusion.80
  556.0 5.7 fusion.79
  561.7 6.5 convolution_bitcast_fusion.4
  568.2 2.9 copy.35
  571.1 35.3 %all_to_all.69 = f32[32,64,256]{2,1,0:T(8,128)} all-to-all(f32[32,64,256]{2,1,0:T(8,128)} %bitcast.85), channel_id=1, replica_groups=mesh['group'=8,'dev'=32] {'dev'}, dimensions={0} | all-to-all | bytes 4194304 | tf_op jit(solution)/shard_map/cond/branch_0_fun/while/body/eval_jaxpr/all_to_all | solution.py:494
  609.6 4.7 all-to-all-start.1
  614.4 28.0 %all-to-all-done.1 = f32[32,64,256]{2,1,0:T(8,128)} async-done(((f32[32,64,256]{2,1,0:T(8,128)}), f32[32,64,256]{2,1,0:T(8,128)}, u32[]{:S(2)}, u32[]{:S(2)}) %all-to-all-start.1) | async-done | bytes 2097184 | tf_op jit(solution)/shard_map/cond/branch_0_fun/while/body/eval_jaxpr/all_to_all | solution.py:496
  642.4 5.7 convolution_bitcast_fusion.5.k_ref
  648.1 7.9 eval_jaxpr.3
  655.9 4.7 fusion.80
  660.7 5.7 fusion.79
  666.3 6.5 convolution_bitcast_fusion.4
  672.8 2.9 copy.35
  675.7 35.3 %all_to_all.69 = f32[32,64,256]{2,1,0:T(8,128)} all-to-all(f32[32,64,256]{2,1,0:T(8,128)} %bitcast.85), channel_id=1, replica_groups=mesh['group'=8,'dev'=32] {'dev'}, dimensions={0} | all-to-all | bytes 4194304 | tf_op jit(solution)/shard_map/cond/branch_0_fun/while/body/eval_jaxpr/all_to_all | solution.py:494
  714.3 4.7 all-to-all-start.1
  719.0 28.0 %all-to-all-done.1 = f32[32,64,256]{2,1,0:T(8,128)} async-done(((f32[32,64,256]{2,1,0:T(8,128)}), f32[32,64,256]{2,1,0:T(8,128)}, u32[]{:S(2)}, u32[]{:S(2)}) %all-to-all-start.1) | async-done | bytes 2097184 | tf_op jit(solution)/shard_map/cond/branch_0_fun/while/body/eval_jaxpr/all_to_all | solution.py:496
  747.0 5.7 convolution_bitcast_fusion.5.k_ref
  752.7 7.9 eval_jaxpr.3
  760.6 4.7 fusion.80
  765.5 5.7 multiply_reduce_fusion
  771.2 12.4 %all_to_all.67 = f32[32,1,256]{2,1,0:T(1,128)S(1)} all-to-all(f32[32,1,256]{2,1,0:T(1,128)S(1)} %broadcast_in_dim.0), channel_id=1, replica_groups=mesh['group'=8,'dev'=32] {'dev'}, dimensions={0} | all-to-all | bytes 65536 | tf_op jit(solution)/shard_map/cond/branch_0_fun/all_to_all | solution.py:494
  783.6 10.7 %all_to_all.68 = f32[32,1,256]{2,1,0:T(1,128)S(1)} all-to-all(f32[32,1,256]{2,1,0:T(1,128)S(1)} %tile.4), channel_id=1, replica_groups=mesh['group'=8,'dev'=32] {'dev'}, dimensions={0} | all-to-all | bytes 65536 | tf_op jit(solution)/shard_map/cond/branch_0_fun/all_to_all | solution.py:496
  794.4 3.2 fusion.3
  797.6 4.6 all-to-all-start.8
  803.1 16.5 %all-to-all-done.8 = f32[32,32,256]{2,1,0:T(8,128)} async-done(((f32[32,32,256]{2,1,0:T(8,128)}), f32[32,32,256]{2,1,0:T(8,128)}, u32[]{:S(2)}, u32[]{:S(2)}) %all-to-all-start.8) | async-done | bytes 1048608 | tf_op jit(solution)/shard_map/cond/branch_0_fun/all_to_all | solution.py:494
  (31 shorter events, 18.9 us)
Async XLA Ops:
  0.6 1.8 copy-start
  0.6 4.5 copy-start.2
  0.7 4.5 copy-start.3
  2.4 3.2 copy-start.4
  220.8 3.8 copy-start.1
  284.3 55.2 %all-to-all-start.4 = ((f32[32,32,1024]{2,1,0:T(8,128)}), f32[32,32,1024]{2,1,0:T(8,128)}, u32[]{:S(2)}, u32[]{:S(2)}) async-start(f32[32,32,1024]{2,1,0:T(8,128)} %tile.1), calls=%async_computation.4 | async-start | bytes 8388608 | tf_op jit(solution)/shard_map/cond/branch_0_fun/all_to_all | solution.py:496
  395.9 52.6 %all-to-all-start.5 = ((f32[8,256,256]{2,1,0:T(8,128)}), f32[8,256,256]{2,1,0:T(8,128)}, u32[]{:S(2)}, u32[]{:S(2)}) async-start(f32[8,256,256]{2,1,0:T(8,128)} %tile.2), calls=%async_computation.5 | async-start | bytes 4194304 | tf_op jit(solution)/shard_map/cond/branch_0_fun/all_to_all | solution.py:496
  505.0 32.7 %all-to-all-start.1 = ((f32[32,64,256]{2,1,0:T(8,128)}), f32[32,64,256]{2,1,0:T(8,128)}, u32[]{:S(2)}, u32[]{:S(2)}) async-start(f32[32,64,256]{2,1,0:T(8,128)} %tile.9), calls=%async_computation.1 | async-start | bytes 4194304 | tf_op jit(solution)/shard_map/cond/branch_0_fun/while/body/eval_jaxpr/all_to_all | solution.py:496
  609.6 32.7 %all-to-all-start.1 = ((f32[32,64,256]{2,1,0:T(8,128)}), f32[32,64,256]{2,1,0:T(8,128)}, u32[]{:S(2)}, u32[]{:S(2)}) async-start(f32[32,64,256]{2,1,0:T(8,128)} %tile.9), calls=%async_computation.1 | async-start | bytes 4194304 | tf_op jit(solution)/shard_map/cond/branch_0_fun/while/body/eval_jaxpr/all_to_all | solution.py:496
  714.3 32.7 %all-to-all-start.1 = ((f32[32,64,256]{2,1,0:T(8,128)}), f32[32,64,256]{2,1,0:T(8,128)}, u32[]{:S(2)}, u32[]{:S(2)}) async-start(f32[32,64,256]{2,1,0:T(8,128)} %tile.9), calls=%async_computation.1 | async-start | bytes 4194304 | tf_op jit(solution)/shard_map/cond/branch_0_fun/while/body/eval_jaxpr/all_to_all | solution.py:496
  797.6 22.0 %all-to-all-start.8 = ((f32[32,32,256]{2,1,0:T(8,128)}), f32[32,32,256]{2,1,0:T(8,128)}, u32[]{:S(2)}, u32[]{:S(2)}) async-start(f32[32,32,256]{2,1,0:T(8,128)} %fusion.3), calls=%async_computation.8 | async-start | bytes 2097152 | tf_op jit(solution)/shard_map/cond/branch_0_fun/all_to_all | solution.py:494
